TPU v7x, 32 devices: a whole 2x2x4 slice. The times are simulated.
32 devices in a mesh: doc: 4 (over z), fsdp: 8 (over y, x, core).
Axes of the slice: x: 2, y: 2, z: 4, core: 2. Of those that a mesh axis runs over, the one named last changes fastest.
Arguments:
- tokens_in: bfloat16 [4, 256, 4096], P('doc'), may hold values from -6 to 6
- mix_in: bfloat16 [4, 256, 8192], P('doc', None, 'fsdp'), may hold values from -6 to 6
- step_size: float32 [4, 256, 128], P('doc', None, 'fsdp'), may hold values from 0.0025 to 0.03
- doc_ids: int32 [4, 256], P('doc'), may hold values from 0 to 3, never falling along the last dimension, each value on 1 to 128 neighbouring positions
- out_grad: bfloat16 [4, 256, 8192], P('doc', None, 'fsdp'), may hold values from -6 to 6
- proj_weight: bfloat16 [4096, 256], P('fsdp'), may hold values from -0.046875 to 0.046875
- conv_weight: float32 [4, 8192], P(None, 'fsdp'), may hold values from -3 to 3
- decay_rate: float32 [128], P('fsdp'), may hold values from 0.02 to 2.5
- carried_state: bfloat16 [4, 128, 64, 128], P(None, 'fsdp', 'doc'), may hold values from -3 to 3
- carried_conv: bfloat16 [4, 3, 128, 64], P(None, None, 'fsdp', 'doc'), may hold values from -6 to 6
- carry_from: int32 [4], replicated, may hold values from -1 to 3, as said below
Outputs:
- grad_proj: float32 [4096, 256], P(('doc', 'fsdp'))
- grad_state: bfloat16 [4, 128, 64, 128], P(None, 'fsdp', 'doc')
- grad_conv: bfloat16 [4, 3, 128, 64], P(None, None, 'fsdp', 'doc')
Inputs may be any that keep to these rules, and one draw needn't show every extreme that they name: `carry_from`: each row names the slot of the previous window that its first document continues, or -1 if it starts fresh; no slot is named by two rows.
All inputs are finite; a program needn't handle non-finite values.
Results may differ from a plain program's by a relative error of at most 0.007.
Values may be sent and summed in bfloat16 or wider, within the bound.
A program may use at most 64 MiB of HBM per device.

v0:
```python
import jax
import jax.numpy as jnp
from jax import lax
from jax.sharding import PartitionSpec as P


def silu_slope(value):
    sigmoid_value = jax.nn.sigmoid(value)
    return sigmoid_value * (1.0 + value * (1.0 - sigmoid_value))


def conv_masks(seg_row, tap_count):
    length = seg_row.shape[0]
    opening = seg_row == seg_row[0]
    tap_masks = []
    for offset in range(tap_count):
        earlier = jnp.concatenate([jnp.full((offset,), -1, jnp.int32), seg_row[: length - offset]])
        inside = jnp.arange(length) >= offset
        tap_masks.append(jnp.where(inside, earlier == seg_row, opening))
    return (opening, tap_masks)


def row_pass(
    coeff, mix_row, step_row, seg_row, grad_rows, state_zero, conv_zero, conv_weight, decay_rate
):
    length, channels = mix_row.shape
    head_count = step_row.shape[1]
    head_dim = channels // head_count
    tap_count = conv_weight.shape[0]
    nstate = coeff.shape[1] // 2
    opening, tap_masks = conv_masks(seg_row, tap_count)
    extended = jnp.concatenate([conv_zero, mix_row], axis=0).astype(jnp.float32)
    preact = jnp.zeros((length, channels), jnp.float32)
    for offset in range(tap_count):
        window = extended[tap_count - 1 - offset : tap_count - 1 - offset + length]
        preact = preact + jnp.where(
            tap_masks[offset][:, None], conv_weight[offset][None, :] * window, 0.0
        )
    mixed_rows = jax.nn.silu(preact).astype(jnp.bfloat16)
    values = (
        step_row[:, :, None] * mixed_rows.reshape(length, head_count, head_dim).astype(jnp.float32)
    ).astype(jnp.bfloat16)
    write_coeff = coeff[:, :nstate]
    read_coeff = coeff[:, nstate:]
    scores = jnp.dot(read_coeff, write_coeff.T, preferred_element_type=jnp.float32)
    log_decay = jnp.cumsum(-(decay_rate[None, :] * step_row), axis=0).T
    lower = jnp.arange(length)[:, None] >= jnp.arange(length)[None, :]
    allowed = lower & (seg_row[:, None] == seg_row[None, :])
    spread = log_decay[:, :, None] - log_decay[:, None, :]
    decays = jnp.where(allowed[None], jnp.exp(jnp.where(allowed[None], spread, 0.0)), 0.0)
    edge_weight = jnp.where(opening[None, :], jnp.exp(log_decay), 0.0)
    weighted = (decays * scores[None]).astype(jnp.bfloat16)
    grad_heads = grad_rows.reshape(length, head_count, head_dim)
    values_grad = jnp.einsum(
        "hts,thp->shp", weighted, grad_heads, preferred_element_type=jnp.float32
    )
    products = jnp.einsum("thp,shp->hts", grad_heads, values, preferred_element_type=jnp.float32)
    score_grad = jnp.sum(decays * products, axis=0)
    carried = jnp.einsum("thp,hpn->thn", grad_heads, state_zero, preferred_element_type=jnp.float32)
    read_grad = jnp.dot(
        score_grad, write_coeff.astype(jnp.float32), precision=lax.Precision.HIGHEST
    )
    read_grad = read_grad + jnp.sum(edge_weight.T[:, :, None] * carried, axis=1)
    write_grad = jnp.dot(
        score_grad.T, read_coeff.astype(jnp.float32), precision=lax.Precision.HIGHEST
    )
    scaled = edge_weight.T[:, :, None] * grad_heads.astype(jnp.float32)
    state_grad = jnp.einsum(
        "thp,tn->hpn", scaled, read_coeff.astype(jnp.float32), precision=lax.Precision.HIGHEST
    )
    mixed_grad = (values_grad * step_row[:, :, None]).reshape(length, channels)
    preact_grad = mixed_grad * silu_slope(preact)
    conv_rows = []
    for index_row in range(tap_count - 1):
        running = jnp.zeros((channels,), jnp.float32)
        for offset in range(tap_count - 1 - index_row, tap_count):
            position = index_row - (tap_count - 1) + offset
            running = running + jnp.where(
                opening[position], conv_weight[offset] * preact_grad[position], 0.0
            )
        conv_rows.append(running)
    conv_grad = jnp.stack(conv_rows)
    return (jnp.concatenate([write_grad, read_grad], axis=1), state_grad, conv_grad)


def shards(
    tokens_in,
    mix_in,
    step_size,
    doc_ids,
    out_grad,
    proj_weight,
    conv_weight,
    decay_rate,
    carried_state,
    carried_conv,
    carry_from,
):
    rows_dev, length, model_width = tokens_in.shape
    head_count = step_size.shape[2]
    slot_count = carried_state.shape[0]
    part_p = carried_state.shape[2]
    nstate = carried_state.shape[3]
    tap_count = conv_weight.shape[0]
    doc_count = lax.axis_size("doc")
    head_dim = part_p * doc_count
    channels = head_count * head_dim
    picker = (carry_from[:, None] == jnp.arange(slot_count, dtype=jnp.int32)[None, :]).astype(
        jnp.bfloat16
    )
    chosen_state = jnp.einsum(
        "rs,shpn->rhpn", picker, carried_state, preferred_element_type=jnp.float32
    ).astype(jnp.bfloat16)
    chosen_conv = jnp.einsum(
        "rs,skhp->rkhp", picker, carried_conv, preferred_element_type=jnp.float32
    ).astype(jnp.bfloat16)
    chosen_state = chosen_state.reshape(slot_count, head_count, part_p * nstate)
    chosen_conv = chosen_conv.reshape(slot_count, (tap_count - 1) * head_count, part_p)
    start_state, start_conv = (
        lax.all_to_all(chosen_state, "doc", split_axis=0, concat_axis=2, tiled=True),
        lax.all_to_all(chosen_conv, "doc", split_axis=0, concat_axis=2, tiled=True),
    )
    start_state = start_state.reshape(rows_dev, head_count, head_dim, nstate)
    start_conv = start_conv.reshape(rows_dev, tap_count - 1, channels)
    flattened = tokens_in.reshape(rows_dev * length, model_width)
    coeff_sum = jnp.dot(
        flattened,
        lax.all_gather(proj_weight, "fsdp", axis=0, tiled=True),
        preferred_element_type=jnp.float32,
    )
    coeff = coeff_sum.astype(jnp.bfloat16).reshape(rows_dev, length, proj_weight.shape[1])
    coeff_grad, state_grad, conv_grad = row_pass(
        coeff[0],
        mix_in[0],
        step_size[0],
        doc_ids[0],
        out_grad[0],
        start_state[0],
        start_conv[0],
        conv_weight,
        decay_rate,
    )
    coeff_grads = [coeff_grad]
    state_grads = [state_grad]
    conv_grads = [conv_grad]
    back_state = (
        jnp.stack(state_grads).astype(jnp.bfloat16).reshape(rows_dev, head_count, head_dim * nstate)
    )
    back_conv = (
        jnp.stack(conv_grads)
        .astype(jnp.bfloat16)
        .reshape(rows_dev, (tap_count - 1) * head_count, head_dim)
    )
    got_state, got_conv = (
        lax.all_to_all(back_state, "doc", split_axis=2, concat_axis=0, tiled=True),
        lax.all_to_all(back_conv, "doc", split_axis=2, concat_axis=0, tiled=True),
    )
    grad_state = jnp.einsum(
        "rs,rx->sx", picker, got_state.reshape(slot_count, -1), preferred_element_type=jnp.float32
    )
    grad_state = grad_state.astype(jnp.bfloat16).reshape(carried_state.shape)
    grad_conv = jnp.einsum(
        "rs,rx->sx", picker, got_conv.reshape(slot_count, -1), preferred_element_type=jnp.float32
    )
    grad_conv = grad_conv.astype(jnp.bfloat16).reshape(carried_conv.shape)
    coeff_flat = jnp.stack(coeff_grads).reshape(rows_dev * length, -1)
    share = lax.psum_scatter(coeff_flat, "fsdp", scatter_dimension=1, tiled=True)
    partial_cols = jnp.einsum(
        "tj,tn->jn", flattened.astype(jnp.float32), share, precision=lax.Precision.HIGHEST
    )
    summed_cols = lax.psum_scatter(partial_cols, "doc", scatter_dimension=0, tiled=True)
    grad_proj = lax.all_to_all(summed_cols, "fsdp", split_axis=0, concat_axis=1, tiled=True)
    return (grad_proj, grad_state, grad_conv)


def solution(mesh):
    return jax.shard_map(
        shards,
        mesh=mesh,
        in_specs=(
            P("doc", None, None),
            P("doc", None, "fsdp"),
            P("doc", None, "fsdp"),
            P("doc", None),
            P("doc", None, "fsdp"),
            P("fsdp", None),
            P(None, "fsdp"),
            P("fsdp"),
            P(None, "fsdp", "doc", None),
            P(None, None, "fsdp", "doc"),
            P(),
        ),
        out_specs=(
            P(("doc", "fsdp"), None),
            P(None, "fsdp", "doc", None),
            P(None, None, "fsdp", "doc"),
        ),
        check_vma=False,
    )
```

profile of v0, /device:TPU:0, one launch (start us, length us, event | category | flops | bytes accessed | tf_op | source)
XLA Modules:
  0.0 206.1 jit_solution(14313732095959706522)
XLA Ops:
  7.9 1.1 convolution_convert_fusion.3
  9.8 6.3 %all-to-all-start = ((bf16[4,2,384]{2,1,0:T(2,128)(2,1)}), bf16[4,2,384]{2,1,0:T(2,128)(2,1)S(1)}, u32[]{:S(2)}, u32[]{:S(2)}) async-start(bf16[4,2,384]{2,1,0:T(2,128)(2,1)} %reshape.194), calls=%async_computation | async-start | bytes 12288 | tf_op jit(solution)/shard_map/all_to_all | solution.py:121
  16.1 1.2 slice.91
  18.9 1.4 compare_reduce_fusion
  21.9 1.3 convolution_convert_fusion.2
  25.0 5.1 %all-to-all-start.1 = ((bf16[4,16,2048]{2,1,0:T(8,128)(2,1)}), bf16[4,16,2048]{2,1,0:T(8,128)(2,1)S(1)}, u32[]{:S(2)}, u32[]{:S(2)}) async-start(bf16[4,16,2048]{2,1,0:T(8,128)(2,1)} %reshape.182), calls=%async_computation.1 | async-start | bytes 524288 | tf_op jit(solution)/shard_map/all_to_all | solution.py:120
  30.1 1.3 broadcast_compare_fusion
  31.5 1.0 copy.78
  32.8 1.2 maximum_convert_fusion
  34.0 4.4 %all-to-all-done.1 = bf16[4,16,2048]{2,1,0:T(8,128)(2,1)S(1)} async-done(((bf16[4,16,2048]{2,1,0:T(8,128)(2,1)}), bf16[4,16,2048]{2,1,0:T(8,128)(2,1)S(1)}, u32[]{:S(2)}, u32[]{:S(2)}) %all-to-all-start.1) | async-done | bytes 262176 | tf_op jit(solution)/shard_map/all_to_all | solution.py:120
  39.3 1.1 squeeze_reshape.7
  40.5 2.2 %fusion.2 = f32[256,128]{0,1:T(8,128)} fusion(bf16[16,64,128]{2,1,0:T(8,128)(2,1)S(1)} %squeeze_reshape.7, bf16[256,16,64]{0,2,1:T(8,128)(2,1)} %bitcast.125, f32[256,16]{0,1:T(8,128)S(1)} %select_bitcast_fusion), kind=kOutput, calls=%fused_computation.8 | convolution fusion | flops 68124672 | bytes 933888 | tf_op jit(solution)/shard_map/thp,hpn->thn/dot_general | solution.py:59
  42.7 2.4 %fusion.14 = bf16[256,256]{1,0:T(8,128)(2,1)S(1)} fusion(bf16[4096,256]{1,0:T(8,128)(2,1)} %all-gather.2.cloned.1.call-done, bf16[1,256,4096]{2,1,0:T(8,128)(2,1)S(1)} %copy-done), kind=kOutput, calls=%fused_computation.22 | convolution fusion | flops 536936448 | bytes 4325376 | tf_op jit(solution)/shard_map/dot_general | solution.py:126
  45.3 2.4 %fusion.12 = f32[256,16,64]{0,2,1:T(8,128)} fusion(bf16[256,16,64]{0,2,1:T(8,128)(2,1)S(1)} %bitcast.127, f32[256,256]{0,1:T(8,128)S(1)} %fusion.31, f32[16,256]{1,0:T(8,128)S(1)} %copy-done.8, pred[256,256]{0,1:T(8,128)(4,1)S(1)} %fusion.29, f32[256,16]{0,1:T(8,128)S(1)} %bitcast.150), kind=kOutput, calls=%fused_computation.18 | convolution fusion | flops 139722752 | bytes 1933312 | tf_op jit(solution)/shard_map/hts,thp->shp/dot_general | solution.py:54
  47.7 2.5 %copy.87 = f32[256,1024]{1,0:T(8,128)} copy(f32[256,1024]{0,1:T(8,128)} %bitcast.130) | data formatting | bytes 2097152 | tf_op jit(solution)/shard_map/reshape | solution.py:71
  50.2 3.1 %multiply_multiply_fusion = (f32[256,1024]{1,0:T(8,128)}, f32[256,1024]{1,0:T(8,128)S(1)}) fusion(f32[256,1024]{1,0:T(8,128)} %copy.87, f32[259,1024]{1,0:T(8,128)S(1)} %maximum_convert_fusion, f32[1024]{0:T(1024)S(1)} %bitcast.148, pred[256]{0:T(512)(128)(4,1)S(1)} %copy-done.10, f32[1024]{0:T(1024)S(1)} %bitcast.149, ...), kind=kLoop, calls=%fused_computation.36 | loop fusion | flops 4718592 | bytes 7357184 | tf_op jit(solution)/shard_map/mul | solution.py:72
  53.6 1.4 copy.77
  55.0 2.9 %fusion = f32[256,256]{0,1:T(8,128)S(1)} fusion(bf16[256,16,64]{0,2,1:T(8,128)(2,1)} %bitcast.126, f32[16,256]{1,0:T(8,128)S(1)} %copy-done.8, pred[256,256]{0,1:T(8,128)(4,1)S(1)} %fusion.29, f32[256,16,64]{0,2,1:T(8,128)} %bitcast.129, f32[256,16]{0,1:T(8,128)S(1)} %bitcast.151), kind=kOutput, calls=%fused_computation.3 | convolution fusion | flops 139919360 | bytes 1933312 | tf_op jit(solution)/shard_map/thp,shp->hts/dot_general | solution.py:57
  59.3 32.8 %reduce-scatter.3.cloned.1.call-done = f32[256,32]{0,1:T(8,128)} async-done(((f32[256,256]{0,1:T(8,128)}), f32[256,32]{0,1:T(8,128)}) %reduce-scatter.3.cloned.1.call-update) | async-done | bytes 32784 | tf_op jit(solution)/shard_map/reduce_scatter | solution.py:167
  92.1 2.7 %convolution_bitcast_fusion = f32[4096,32]{0,1:T(8,128)} fusion(f32[256,32]{0,1:T(8,128)} %reduce-scatter.3.cloned.1.call-done, bf16[1,256,4096]{2,1,0:T(8,128)(2,1)S(1)} %copy-done), kind=kOutput, calls=%fused_computation.1 | convolution fusion | flops 402653184 | bytes 2654208 | tf_op jit(solution)/shard_map/tj,tn->jn/dot_general | solution.py:168
  95.4 2.8 %fusion.40 = (bf16[1,1,1024]{2,1,0:T(2,128)(2,1)S(1)}, bf16[1,1,1024]{2,1,0:T(2,128)(2,1)S(1)}, bf16[1,1,1024]{2,1,0:T(2,128)(2,1)S(1)}) fusion(pred[]{:T(512)} %bitcast.32, f32[256,1024]{1,0:T(8,128)} %get-tuple-element.15, f32[4,1024]{1,0:T(4,128)S(1)} %copy-done.6, pred[]{:T(512)} %bitcast.36, pred[]{:T(512)} %bitcast.38), kind=kLoop, calls=%fused_computation.74 | loop fusion | flops 18432 | bytes 30723 | tf_op jit(solution)/shard_map/stack | solution.py:82
  100.4 4.6 %all-to-all-start.4 = ((bf16[4,2,384]{2,1,0:T(2,128)(2,1)}), bf16[4,2,384]{2,1,0:T(2,128)(2,1)S(1)}, u32[]{:S(2)}, u32[]{:S(2)}) async-start(bf16[4,2,384]{2,1,0:T(2,128)(2,1)} %reshape.198), calls=%async_computation.6 | async-start | bytes 12288 | tf_op jit(solution)/shard_map/all_to_all | solution.py:156
  105.8 6.7 %copy.83 = bf16[1,16,8192]{1,0,2:T(2,128)(2,1)} copy(bf16[1,16,8192]{2,1,0:T(8,128)(2,1)S(1)} %reshape.183) | data formatting | bytes 524288 | tf_op jit(solution)/shard_map/reshape | solution.py:147
  112.5 46.5 %reduce.4 = bf16[8192,16]{1,0:T(8,128)(2,1)} reduce(bf16[8192,1,16]{2,1,0:T(2,128)(2,1)} %bitcast.123, bf16[]{:T(256)} %broadcast.77), dimensions={1}, to_apply=%bitcast.98.reduce_sub_computation | reduce | bytes 524290
  159.1 4.1 %reshape.196 = bf16[4,2,16384]{2,1,0:T(2,128)(2,1)} reshape(bf16[8192,16]{1,0:T(8,128)(2,1)} %reduce.4) | data formatting | bytes 524288
  163.1 5.1 %all-to-all-start.3 = ((bf16[4,2,16384]{2,1,0:T(2,128)(2,1)}), bf16[4,2,16384]{2,1,0:T(2,128)(2,1)S(1)}, u32[]{:S(2)}, u32[]{:S(2)}) async-start(bf16[4,2,16384]{2,1,0:T(2,128)(2,1)} %reshape.196), calls=%async_computation.5 | async-start | bytes 524288 | tf_op jit(solution)/shard_map/all_to_all | solution.py:155
  169.6 6.7 %all-to-all-done.3 = bf16[4,2,16384]{2,1,0:T(2,128)(2,1)S(1)} async-done(((bf16[4,2,16384]{2,1,0:T(2,128)(2,1)}), bf16[4,2,16384]{2,1,0:T(2,128)(2,1)S(1)}, u32[]{:S(2)}, u32[]{:S(2)}) %all-to-all-start.3) | async-done | bytes 262176 | tf_op jit(solution)/shard_map/all_to_all | solution.py:155
  176.3 4.1 %reshape.197 = bf16[8192,1,16]{2,1,0:T(2,128)(2,1)} reshape(bf16[4,2,16384]{2,1,0:T(2,128)(2,1)S(1)} %all-to-all-done.3) | data formatting | bytes 524288
  180.3 7.9 %copy.84 = bf16[1,16,8192]{2,1,0:T(8,128)(2,1)S(1)} copy(bf16[1,16,8192]{1,0,2:T(2,128)(2,1)} %bitcast.124) | data formatting | bytes 524288 | tf_op jit(solution)/shard_map/all_to_all | solution.py:155
  188.4 1.6 copy_bitcast_fusion
  190.0 3.4 %all-to-all-start.2 = ((f32[8,128,32]{1,2,0:T(8,128)}), f32[8,128,32]{1,2,0:T(8,128)S(1)}, u32[]{:S(2)}, u32[]{:S(2)}) async-start(f32[8,128,32]{1,2,0:T(8,128)} %copy_bitcast_fusion), calls=%async_computation.4 | async-start | bytes 262144 | tf_op jit(solution)/shard_map/all_to_all | solution.py:172
  194.5 4.3 %all-to-all-done.2 = f32[8,128,32]{1,2,0:T(8,128)S(1)} async-done(((f32[8,128,32]{1,2,0:T(8,128)}), f32[8,128,32]{1,2,0:T(8,128)S(1)}, u32[]{:S(2)}, u32[]{:S(2)}) %all-to-all-start.2) | async-done | bytes 131104 | tf_op jit(solution)/shard_map/all_to_all | solution.py:172
  (76 shorter events, 16.5 us)
Async XLA Ops:
  7.2 35.5 %copy-start = (bf16[1,256,4096]{2,1,0:T(8,128)(2,1)S(1)}, bf16[1,256,4096]{2,1,0:T(8,128)(2,1)}, u32[]{:S(2)}) copy-start(bf16[1,256,4096]{2,1,0:T(8,128)(2,1)} %param.11) | copy-start | bytes 6291460
  7.2 22.9 %copy-start.5 = (s32[1,256]{1,0:T(1,128)S(1)}, s32[1,256]{1,0:T(1,128)}, u32[]{:S(2)}) copy-start(s32[1,256]{1,0:T(1,128)} %param.14) | copy-start | bytes 3076
  7.2 24.3 %copy-start.3 = (bf16[1,256,1024]{2,1,0:T(8,128)(2,1)S(1)}, bf16[1,256,1024]{2,1,0:T(8,128)(2,1)}, u32[]{:S(2)}) copy-start(bf16[1,256,1024]{2,1,0:T(8,128)(2,1)} %param.15) | copy-start | bytes 1572868
  7.2 35.5 %all-gather.2.cloned.1.call-start = ((), (), s32[]{:S(2)}) async-start(), calls=%async_computation.7 | async-start | bytes 2359296 | tf_op jit(solution)/shard_map/all_gather | solution.py:128
  9.8 15.2 %all-to-all-start = ((bf16[4,2,384]{2,1,0:T(2,128)(2,1)}), bf16[4,2,384]{2,1,0:T(2,128)(2,1)S(1)}, u32[]{:S(2)}, u32[]{:S(2)}) async-start(bf16[4,2,384]{2,1,0:T(2,128)(2,1)} %reshape.194), calls=%async_computation | async-start | bytes 12288 | tf_op jit(solution)/shard_map/all_to_all | solution.py:121
  25.0 13.4 %all-to-all-start.1 = ((bf16[4,16,2048]{2,1,0:T(8,128)(2,1)}), bf16[4,16,2048]{2,1,0:T(8,128)(2,1)S(1)}, u32[]{:S(2)}, u32[]{:S(2)}) async-start(bf16[4,16,2048]{2,1,0:T(8,128)(2,1)} %reshape.182), calls=%async_computation.1 | async-start | bytes 524288 | tf_op jit(solution)/shard_map/all_to_all | solution.py:120
  30.1 62.0 %reduce-scatter.3.cloned.1.call-start = ((), (), s32[]{:S(2)}) async-start(), calls=%async_computation.8 | async-start | bytes 294912 | tf_op jit(solution)/shard_map/reduce_scatter | solution.py:167
  42.7 2.6 %copy-start.7 = (f32[1,256,16]{1,2,0:T(8,128)S(1)}, f32[1,256,16]{1,2,0:T(8,128)}, u32[]{:S(2)}) copy-start(f32[1,256,16]{1,2,0:T(8,128)} %param.13) | copy-start | bytes 49156
  42.7 2.6 %copy-start.8 = (f32[16,256]{1,0:T(8,128)S(1)}, f32[16,256]{1,0:T(8,128)}, u32[]{:S(2)}) copy-start(f32[16,256]{1,0:T(8,128)} %copy_bitcast_fusion.1) | copy-start | bytes 49156
  42.7 2.6 %copy-start.1 = (bf16[1,256,1024]{1,2,0:T(8,128)(2,1)S(1)}, bf16[1,256,1024]{1,2,0:T(8,128)(2,1)}, u32[]{:S(2)}) copy-start(bf16[1,256,1024]{1,2,0:T(8,128)(2,1)} %copy.78) | copy-start | bytes 1572868
  47.7 2.5 %copy-start.9 = (pred[256]{0:T(512)(128)(4,1)S(1)}, pred[256]{0:T(512)(128)(4,1)}, u32[]{:S(2)}) copy-start(pred[256]{0:T(512)(128)(4,1)} %get-tuple-element.26) | copy-start | bytes 772
  47.7 2.5 %copy-start.10 = (pred[256]{0:T(512)(128)(4,1)S(1)}, pred[256]{0:T(512)(128)(4,1)}, u32[]{:S(2)}) copy-start(pred[256]{0:T(512)(128)(4,1)} %get-tuple-element.27) | copy-start | bytes 772
  55.0 3.2 %copy-start.4 = (f32[256,128]{0,1:T(8,128)S(1)}, f32[256,128]{0,1:T(8,128)}, u32[]{:S(2)}) copy-start(f32[256,128]{0,1:T(8,128)} %fusion.2) | copy-start | bytes 393220
  58.5 36.9 %copy-start.6 = (f32[4,1024]{1,0:T(4,128)S(1)}, f32[4,1024]{1,0:T(4,128)}, u32[]{:S(2)}) copy-start(f32[4,1024]{1,0:T(4,128)} %param.17) | copy-start | bytes 49156
  58.5 46.5 %copy-start.2 = (bf16[1,256,1024]{1,2,0:T(8,128)(2,1)S(1)}, bf16[1,256,1024]{1,2,0:T(8,128)(2,1)}, u32[]{:S(2)}) copy-start(bf16[1,256,1024]{1,2,0:T(8,128)(2,1)} %copy.78) | copy-start | bytes 1572868
  59.2 129.2 %reduce-scatter.5.cloned.1.call-start = ((), (), s32[]{:S(2)}) async-start(), calls=%async_computation.9 | async-start | bytes 655360 | tf_op jit(solution)/shard_map/reduce_scatter | solution.py:171
  100.4 62.7 %all-to-all-start.4 = ((bf16[4,2,384]{2,1,0:T(2,128)(2,1)}), bf16[4,2,384]{2,1,0:T(2,128)(2,1)S(1)}, u32[]{:S(2)}, u32[]{:S(2)}) async-start(bf16[4,2,384]{2,1,0:T(2,128)(2,1)} %reshape.198), calls=%async_computation.6 | async-start | bytes 12288 | tf_op jit(solution)/shard_map/all_to_all | solution.py:156
  159.1 9.5 %copy-start.11 = (s32[4]{0:T(128)S(1)}, s32[4]{0:T(128)}, u32[]{:S(2)}) copy-start(s32[4]{0:T(128)} %param.21) | copy-start | bytes 52
  163.1 13.1 %all-to-all-start.3 = ((bf16[4,2,16384]{2,1,0:T(2,128)(2,1)}), bf16[4,2,16384]{2,1,0:T(2,128)(2,1)S(1)}, u32[]{:S(2)}, u32[]{:S(2)}) async-start(bf16[4,2,16384]{2,1,0:T(2,128)(2,1)} %reshape.196), calls=%async_computation.5 | async-start | bytes 524288 | tf_op jit(solution)/shard_map/all_to_all | solution.py:155
  190.0 8.8 %all-to-all-start.2 = ((f32[8,128,32]{1,2,0:T(8,128)}), f32[8,128,32]{1,2,0:T(8,128)S(1)}, u32[]{:S(2)}, u32[]{:S(2)}) async-start(f32[8,128,32]{1,2,0:T(8,128)} %copy_bitcast_fusion), calls=%async_computation.4 | async-start | bytes 262144 | tf_op jit(solution)/shard_map/all_to_all | solution.py:172
Sparse Core Ops, SparseCore 0:
  9.9 30.7 all-gather.1
  59.4 32.6 reduce-scatter.2
  94.9 21.6 reduce-scatter.4
where the time goes:
time: 207 us; the launch traced here: 206 us
  other arithmetic  61.2 us (30%)
  waiting for transfers between devices  49 us (24%)
  local copies, waits for them, and re-layouts  40.3 us (19%)
  starting transfers between devices  24.6 us (12%)
  matrix products  17 us (8%)
  between operations  14 us (7%)
    unnamed x2, other arithmetic  47.3 us
    reduce_scatter x1, waiting for transfers between devices, shards(): lax.psum_scatter(coeff_flat, 'fsdp', scatter_dimension=1, tiled=True)  32.8 us
    unnamed x35, local copies, waits for them, and re-layouts  12.8 us
    all_to_all x2, local copies, waits for them, and re-layouts, shards(): lax.all_to_all(back_state, 'doc', split_axis=2, concat_axis=0, tiled=True)  8.05 us
    reshape x2, local copies, waits for them, and re-layouts, shards(): jnp.stack(state_grads).astype(jnp.bfloat16)  6.85 us
    all_to_all x1, waiting for transfers between devices, shards(): lax.all_to_all(back_state, 'doc', split_axis=2, concat_axis=0, tiled=True)  6.72 us
    all_to_all x1, starting transfers between devices, shards(): lax.all_to_all(chosen_conv, 'doc', split_axis=0, concat_axis=2, tiled=True)  6.32 us
    all_to_all x1, starting transfers between devices, shards(): lax.all_to_all(back_state, 'doc', split_axis=2, concat_axis=0, tiled=True)  5.09 us
  transfers between devices with their start and end apart: 8, of which 4 were waited for; matrix products, arithmetic and copies ran while one was open for 47% of the time, Pallas kernels for 0%

commit v1 on v0

--- a/solution.py
+++ b/solution.py
@@ -1,6 +1,10 @@
+import functools
+
 import jax
 import jax.numpy as jnp
 from jax import lax
+from jax.experimental import pallas as pl
+from jax.experimental.pallas import tpu as pltpu
 from jax.sharding import PartitionSpec as P
 
 
@@ -173,9 +177,479 @@
     return (grad_proj, grad_state, grad_conv)
 
 
+F32 = jnp.float32
+BF16 = jnp.bfloat16
+MESH = pl.DeviceIdType.MESH
+
+
+def dot_nn(a, b, precision=None):
+    return lax.dot_general(
+        a, b, (((1,), (0,)), ((), ())), precision=precision, preferred_element_type=F32
+    )
+
+
+def dot_nt(a, b):
+    return lax.dot_general(a, b, (((1,), (1,)), ((), ())), preferred_element_type=F32)
+
+
+def dot_tn(a, b):
+    return lax.dot_general(a, b, (((0,), (0,)), ((), ())), preferred_element_type=F32)
+
+
+def iota(shape, axis):
+    return lax.broadcasted_iota(jnp.int32, shape, axis)
+
+
+def layer_kernel(
+    docs,
+    parts,
+    carry_ref,
+    tokens_ref,
+    mix_ref,
+    step_ref,
+    seg_ref,
+    grad_ref,
+    weight_ref,
+    taps_ref,
+    rate_ref,
+    state_ref,
+    conv_ref,
+    proj_out,
+    state_out,
+    conv_out,
+    tok_part,
+    tok_cols,
+    coeff_partial,
+    coeff_recv,
+    coeff,
+    cg_partial,
+    cg_recv,
+    cg,
+    state_send,
+    state_recv,
+    conv_send,
+    conv_recv,
+    sgrad_send,
+    sgrad_recv,
+    cgrad_send,
+    cgrad_recv,
+    fin_own,
+    fin_send,
+    fin_recv,
+    ext,
+    seg_ext,
+    og_scaled,
+    val_scaled,
+    first_pre,
+    first_scale,
+    load_sem,
+    part_send_sem,
+    part_recv_sem,
+    doc_send_sem,
+    doc_recv_sem,
+):
+    d = lax.axis_index("doc")
+    f = lax.axis_index("fsdp")
+    length, channels = mix_ref.shape[1], mix_ref.shape[2]
+    heads = step_ref.shape[2]
+    head_dim = channels // heads
+    part_p = head_dim // docs
+    width = weight_ref.shape[1]
+    nstate = width // 2
+    slots = state_ref.shape[0]
+    depth = weight_ref.shape[0]
+    block = length // parts
+    out_rows = proj_out.shape[0]
+    taps = taps_ref.shape[0]
+
+    loads = [
+        pltpu.make_async_copy(
+            tokens_ref.at[0, :, pl.ds(pl.multiple_of(f * depth, 128), depth)],
+            tok_part,
+            load_sem.at[0],
+        )
+    ]
+    for q in range(docs):
+        loads.append(
+            pltpu.make_async_copy(
+                tokens_ref.at[
+                    0, :, pl.ds(pl.multiple_of((q * parts + f) * out_rows, 128), out_rows)
+                ],
+                tok_cols.at[:, pl.ds(q * out_rows, out_rows)],
+                load_sem.at[1 + q],
+            )
+        )
+    for load in loads:
+        load.start()
+
+    barrier = pltpu.get_barrier_semaphore()
+    for j in range(1, parts):
+        pl.semaphore_signal(
+            barrier, inc=1, device_id=(d, lax.rem(f + j, parts)), device_id_type=MESH
+        )
+    for j in range(1, docs):
+        pl.semaphore_signal(
+            barrier, inc=1, device_id=(lax.rem(d + j, docs), f), device_id_type=MESH
+        )
+
+    def part_copy(phase, j, src, dst):
+        return pltpu.make_async_remote_copy(
+            src_ref=src,
+            dst_ref=dst,
+            send_sem=part_send_sem.at[phase, j],
+            recv_sem=part_recv_sem.at[phase, j],
+            device_id=(d, lax.rem(f + j, parts)),
+            device_id_type=MESH,
+        )
+
+    def doc_copy(phase, j, src, dst):
+        return pltpu.make_async_remote_copy(
+            src_ref=src,
+            dst_ref=dst,
+            send_sem=doc_send_sem.at[phase, j],
+            recv_sem=doc_recv_sem.at[phase, j],
+            device_id=(lax.rem(d + j, docs), f),
+            device_id_type=MESH,
+        )
+
+    def rows_of(owner):
+        return pl.ds(pl.multiple_of(owner * block, block), block)
+
+    for r in range(slots):
+        source = carry_ref[r]
+        usable = jnp.where(source >= 0, 1.0, 0.0)
+        index = jnp.maximum(source, 0)
+        state_send[r] = (state_ref[index].astype(F32) * usable).astype(BF16)
+        conv_send[r] = (conv_ref[index].astype(F32) * usable).astype(BF16)
+
+    loads[0].wait()
+    coeff_partial[...] = dot_nn(tok_part[...], weight_ref[...])
+
+    pl.semaphore_wait(barrier, parts - 1 + docs - 1)
+
+    conv_copies = [
+        doc_copy(0, j, conv_send.at[lax.rem(d + j, docs)], conv_recv.at[d]) for j in range(1, docs)
+    ]
+    coeff_copies = [
+        part_copy(0, j, coeff_partial.at[rows_of(lax.rem(f + j, parts))], coeff_recv.at[j])
+        for j in range(1, parts)
+    ]
+    state_copies = [
+        doc_copy(1, j, state_send.at[lax.rem(d + j, docs)], state_recv.at[:, d])
+        for j in range(1, docs)
+    ]
+    for copy in conv_copies + coeff_copies + state_copies:
+        copy.start()
+    conv_recv[d] = conv_send[d]
+    state_recv[:, d] = state_send[d]
+
+    lower = iota((length, length), 0) >= iota((length, length), 1)
+    steps = step_ref[0]
+    log_decay = dot_nn(
+        jnp.where(lower, 1.0, 0.0), -(rate_ref[...] * steps), precision=lax.Precision.HIGHEST
+    )
+
+    def halves(x):
+        top = x.astype(BF16)
+        return top, (x - top.astype(F32)).astype(BF16)
+
+    grow = halves(jnp.exp(log_decay))
+    shrink = halves(jnp.exp(-log_decay))
+    step_halves = halves(steps)
+
+    seg_row = seg_ref[...].astype(F32)
+    seg_cols = jnp.broadcast_to(seg_row, (128, length)).T
+    seg_ext[8:, :] = seg_cols
+    seg_ext[:8, :] = jnp.broadcast_to(seg_cols[:1], (8, 128))
+    allowed = lower & (seg_cols[:, :1] == seg_row)
+    opening = seg_cols == seg_cols[:1]
+
+    for copy in conv_copies:
+        copy.wait_recv()
+
+    def place(q):
+        lane = iota((part_p, channels), 1)
+        return jnp.where(
+            lax.rem(lane, head_dim) == iota((part_p, channels), 0) + q * part_p, 1.0, 0.0
+        ).astype(BF16)
+
+    places = [place(q) for q in range(docs)]
+    head_rows = (taps - 1) * heads
+    own_head = (
+        lax.div(iota((taps - 1, heads, channels), 2), head_dim)
+        == iota((taps - 1, heads, channels), 1)
+    )
+    spread = jnp.zeros((head_rows, channels), F32)
+    for q in range(docs):
+        spread = spread + dot_nn(conv_recv[q].reshape(head_rows, part_p), places[q])
+    carried_rows = jnp.sum(
+        jnp.where(own_head, spread.reshape(taps - 1, heads, channels), 0.0), axis=1
+    )
+    ext[:8, :] = jnp.zeros((8, channels), F32)
+    ext[8 - (taps - 1) : 8, :] = carried_rows
+    ext[8:, :] = mix_ref[0].astype(F32)
+
+    for copy in coeff_copies:
+        copy.wait_recv()
+    total = coeff_partial[rows_of(f)]
+    for j in range(1, parts):
+        total = total + coeff_recv[j]
+    coeff[rows_of(f)] = total.astype(BF16)
+    gather_copies = [
+        part_copy(1, j, coeff.at[rows_of(f)], coeff.at[rows_of(f)]) for j in range(1, parts)
+    ]
+    for copy in gather_copies:
+        copy.start()
+
+    def chunk(c, carry):
+        lanes = pl.ds(pl.multiple_of(c * 128, 128), 128)
+        expand = jnp.where(
+            iota((heads, 128), 0) == lax.div(iota((heads, 128), 1) + c * 128, head_dim), 1.0, 0.0
+        ).astype(BF16)
+
+        def per_channel(pair):
+            return dot_nn(pair[0], expand) + dot_nn(pair[1], expand)
+
+        preact = jnp.zeros((length, 128), F32)
+        for k in range(taps):
+            same = seg_ext[8 - k : 8 - k + length, :] == seg_cols
+            window = ext[8 - k : 8 - k + length, lanes]
+            preact = preact + jnp.where(same, taps_ref[k : k + 1, lanes] * window, 0.0)
+        step_c = per_channel(step_halves)
+        shrink_c = per_channel(shrink)
+        mixed = (preact / (1.0 + jnp.exp(-preact))).astype(BF16).astype(F32)
+        values = (step_c * mixed).astype(BF16).astype(F32)
+        val_scaled[:, lanes] = (values * shrink_c).astype(BF16)
+        og_scaled[:, lanes] = (grad_ref[0, :, lanes].astype(F32) * per_channel(grow)).astype(BF16)
+        first_pre[:, lanes] = preact[:8]
+        first_scale[:, lanes] = (step_c * shrink_c)[:8]
+        return carry
+
+    lax.fori_loop(0, channels // 128, chunk, 0)
+    score_grad = jnp.where(allowed, dot_nt(og_scaled[...], val_scaled[...]), 0.0).astype(BF16)
+
+    for copy in state_copies:
+        copy.wait_recv()
+    from_state = jnp.where(
+        opening, dot_nn(og_scaled[...], state_recv[...].reshape(channels, nstate)), 0.0
+    )
+
+    for copy in gather_copies:
+        copy.wait_recv()
+    write_coeff = coeff[:, :nstate]
+    read_coeff = coeff[:, nstate:]
+    cg_partial[:, :nstate] = dot_tn(score_grad, read_coeff)
+    cg_partial[:, nstate:] = dot_nn(score_grad, write_coeff) + from_state
+    sum_copies = [
+        part_copy(2, j, cg_partial.at[rows_of(lax.rem(f + j, parts))], cg_recv.at[j])
+        for j in range(1, parts)
+    ]
+    for copy in sum_copies:
+        copy.start()
+
+    open_read = jnp.where(opening, read_coeff.astype(F32), 0.0).astype(BF16)
+    sgrad_send[...] = (
+        dot_tn(og_scaled[...], open_read).astype(BF16).reshape(heads, docs, part_p, nstate)
+    )
+    sgrad_copies = [
+        doc_copy(2, j, sgrad_send.at[:, lax.rem(d + j, docs)], sgrad_recv.at[d])
+        for j in range(1, docs)
+    ]
+    for copy in sgrad_copies:
+        copy.start()
+    first_scores = dot_nt(write_coeff[:16], read_coeff)
+    first_seg = jnp.broadcast_to(seg_row, (16, length)) == seg_cols[:16, :1]
+    first_allowed = first_seg & (iota((16, length), 1) >= iota((16, length), 0))
+    first_scores = jnp.where(first_allowed, first_scores, 0.0).astype(BF16)
+    first_grad = dot_nn(first_scores, og_scaled[...])[:8]
+    pre = first_pre[...]
+    gate = 1.0 / (1.0 + jnp.exp(-pre))
+    pre_grad = first_grad * first_scale[...] * gate * (1.0 + pre * (1.0 - gate))
+    pre_grad = jnp.where(seg_cols[:8, :1] == seg_cols[:1, :1], pre_grad, 0.0)
+    conv_rows = []
+    for row in range(taps - 1):
+        running = jnp.zeros((1, channels), F32)
+        for k in range(taps - 1 - row, taps):
+            position = row - (taps - 1) + k
+            running = running + taps_ref[k : k + 1, :] * pre_grad[position : position + 1]
+        conv_rows.append(
+            jnp.where(own_head[0], jnp.broadcast_to(running, (heads, channels)), 0.0).astype(BF16)
+        )
+    for q in range(docs):
+        for row in range(taps - 1):
+            cgrad_send[q, row] = dot_nt(conv_rows[row], places[q]).astype(BF16)
+    cgrad_copies = [
+        doc_copy(3, j, cgrad_send.at[lax.rem(d + j, docs)], cgrad_recv.at[d])
+        for j in range(1, docs)
+    ]
+    for copy in cgrad_copies:
+        copy.start()
+    sgrad_recv[d] = sgrad_send[:, d]
+    cgrad_recv[d] = cgrad_send[d]
+
+    for copy in sum_copies:
+        copy.wait_recv()
+    total = cg_partial[rows_of(f)]
+    for j in range(1, parts):
+        total = total + cg_recv[j]
+    cg[rows_of(f)] = total.astype(BF16)
+    cg_copies = [part_copy(3, j, cg.at[rows_of(f)], cg.at[rows_of(f)]) for j in range(1, parts)]
+    for copy in cg_copies:
+        copy.start()
+    for load in loads[1:]:
+        load.wait()
+
+    for copy in cg_copies:
+        copy.wait_recv()
+    product = dot_tn(tok_cols[...], cg[...])
+    fin_own[...] = product.reshape(docs, out_rows, width)
+    fin_send[...] = product.astype(BF16).reshape(docs, out_rows, width)
+    fin_copies = [
+        doc_copy(4, j, fin_send.at[lax.rem(d + j, docs)], fin_recv.at[j]) for j in range(1, docs)
+    ]
+    for copy in fin_copies:
+        copy.start()
+
+    for copy in sgrad_copies + cgrad_copies:
+        copy.wait_recv()
+    for s in range(slots):
+        row_of = jnp.int32(0)
+        found = jnp.float32(0.0)
+        for r in range(slots):
+            hit = carry_ref[r] == s
+            row_of = jnp.where(hit, r, row_of)
+            found = jnp.where(hit, 1.0, found)
+        state_out[s] = (sgrad_recv[row_of].astype(F32) * found).astype(BF16)
+        conv_out[s] = (cgrad_recv[row_of].astype(F32) * found).astype(BF16)
+
+    for copy in fin_copies:
+        copy.wait_recv()
+    result = fin_own[d]
+    for j in range(1, docs):
+        result = result + fin_recv[j].astype(F32)
+    proj_out[...] = result
+
+    for copies in (
+        conv_copies,
+        coeff_copies,
+        state_copies,
+        gather_copies,
+        sum_copies,
+        sgrad_copies,
+        cgrad_copies,
+        cg_copies,
+        fin_copies,
+    ):
+        for copy in copies:
+            copy.wait_send()
+
+
+def device_part(docs, parts, *args):
+    (
+        tokens_in,
+        mix_in,
+        step_size,
+        doc_ids,
+        out_grad,
+        proj_weight,
+        conv_weight,
+        decay_rate,
+        carried_state,
+        carried_conv,
+        carry_from,
+    ) = args
+    rows_dev, length, model_width = tokens_in.shape
+    channels = mix_in.shape[2]
+    heads = step_size.shape[2]
+    depth, width = proj_weight.shape
+    slots, _, part_p, nstate = carried_state.shape
+    taps = conv_weight.shape[0]
+    out_rows = model_width // (docs * parts)
+    block = length // parts
+    aligned = (
+        rows_dev == 1
+        and slots == docs
+        and part_p % 16 == 0
+        and heads % 16 == 0
+        and block % 16 == 0
+        and out_rows % 128 == 0
+        and depth % 128 == 0
+        and nstate == 128
+        and channels % 128 == 0
+        and taps <= 8
+    )
+    if not aligned:
+        return shards(*args)
+    vmem = pl.BlockSpec(memory_space=pltpu.VMEM)
+    return pl.pallas_call(
+        functools.partial(layer_kernel, docs, parts),
+        out_shape=(
+            jax.ShapeDtypeStruct((out_rows, width), F32),
+            jax.ShapeDtypeStruct(carried_state.shape, BF16),
+            jax.ShapeDtypeStruct(carried_conv.shape, BF16),
+        ),
+        in_specs=[
+            pl.BlockSpec(memory_space=pltpu.SMEM),
+            pl.BlockSpec(memory_space=pl.ANY),
+        ]
+        + [vmem] * 9,
+        out_specs=(vmem, vmem, vmem),
+        scratch_shapes=[
+            pltpu.VMEM((length, depth), BF16),
+            pltpu.VMEM((length, docs * out_rows), BF16),
+            pltpu.VMEM((length, width), F32),
+            pltpu.VMEM((parts, block, width), F32),
+            pltpu.VMEM((length, width), BF16),
+            pltpu.VMEM((length, width), F32),
+            pltpu.VMEM((parts, block, width), F32),
+            pltpu.VMEM((length, width), BF16),
+            pltpu.VMEM((slots, heads, part_p, nstate), BF16),
+            pltpu.VMEM((heads, docs, part_p, nstate), BF16),
+            pltpu.VMEM((slots, taps - 1, heads, part_p), BF16),
+            pltpu.VMEM((docs, taps - 1, heads, part_p), BF16),
+            pltpu.VMEM((heads, docs, part_p, nstate), BF16),
+            pltpu.VMEM((docs, heads, part_p, nstate), BF16),
+            pltpu.VMEM((docs, taps - 1, heads, part_p), BF16),
+            pltpu.VMEM((docs, taps - 1, heads, part_p), BF16),
+            pltpu.VMEM((docs, out_rows, width), F32),
+            pltpu.VMEM((docs, out_rows, width), BF16),
+            pltpu.VMEM((docs, out_rows, width), BF16),
+            pltpu.VMEM((length + 8, channels), F32),
+            pltpu.VMEM((length + 8, 128), F32),
+            pltpu.VMEM((length, channels), BF16),
+            pltpu.VMEM((length, channels), BF16),
+            pltpu.VMEM((8, channels), F32),
+            pltpu.VMEM((8, channels), F32),
+            pltpu.SemaphoreType.DMA((1 + docs,)),
+            pltpu.SemaphoreType.DMA((4, parts)),
+            pltpu.SemaphoreType.DMA((4, parts)),
+            pltpu.SemaphoreType.DMA((5, docs)),
+            pltpu.SemaphoreType.DMA((5, docs)),
+        ],
+        compiler_params=pltpu.CompilerParams(
+            collective_id=0, has_side_effects=True, vmem_limit_bytes=40 * 1024 * 1024
+        ),
+        cost_estimate=pl.CostEstimate(
+            flops=2 * length * channels * length * 4, bytes_accessed=4 << 20, transcendentals=0
+        ),
+    )(
+        carry_from,
+        tokens_in,
+        mix_in,
+        step_size,
+        doc_ids,
+        out_grad,
+        proj_weight,
+        conv_weight,
+        decay_rate.reshape(1, heads),
+        carried_state,
+        carried_conv,
+    )
+
+
 def solution(mesh):
     return jax.shard_map(
-        shards,
+        functools.partial(device_part, mesh.shape["doc"], mesh.shape["fsdp"]),
         mesh=mesh,
         in_specs=(
             P("doc", None, None),

time: 207 us -> 44 us (0.21)
  other arithmetic: 61.2 us -> 0 us
  waiting for transfers between devices: 49 us -> 0 us
  Pallas kernels: 0 us -> 31 us
  local copies, waits for them, and re-layouts: 40.3 us -> 11.9 us
  starting transfers between devices: 24.6 us -> 0 us
  matrix products: 17 us -> 0 us
  between operations: 14 us -> 0.66 us
    unnamed x2 -> x0, other arithmetic: 47.3 us -> none
    reduce_scatter x2 -> x0, waiting for transfers between devices: 32.8 us -> none  [the longest x1 32.8 us: shards(): lax.psum_scatter(coeff_flat, 'fsdp', scatter_dimension=1, tiled=True)]
    pallas_call x0 -> x1, Pallas kernels: none -> 31 us  [device_part(): pl.pallas_call(functools.partial(layer_kernel, docs, parts), out_shape=(j...]
    all_to_all x5 -> x0, starting transfers between devices: 24.5 us -> none  [the longest x1 6.32 us: shards(): lax.all_to_all(chosen_conv, 'doc', split_axis=0, concat_axis=2, tiled=True)]
    dot_general x13 -> x0, matrix products: 17 us -> none  [the longest x1 2.89 us: row_pass(): jnp.einsum('thp,shp->hts', grad_heads, values, preferred_element_type=jnp...]
    all_to_all x5 -> x0, waiting for transfers between devices: 15.5 us -> none  [the longest x1 6.72 us: shards(): lax.all_to_all(back_state, 'doc', split_axis=2, concat_axis=0, tiled=True)]
    reshape x7 -> x0, local copies, waits for them, and re-layouts: 11.1 us -> none  [the longest x2 6.85 us: shards(): jnp.stack(state_grads).astype(jnp.bfloat16)]
    all_to_all x7 -> x0, local copies, waits for them, and re-layouts: 10.7 us -> none  [the longest x2 8.05 us: shards(): lax.all_to_all(back_state, 'doc', split_axis=2, concat_axis=0, tiled=True)]
  transfers between devices with their start and end apart: 8 -> 0, of which waited for: 4 -> 0; matrix products, arithmetic and copies ran while one was open for 47% -> 0% of each run, Pallas kernels for 0% -> 0%
where the time goes in v1:
time: 44 us; the launch traced here: 43.5 us
  Pallas kernels  31 us (70%)
  local copies, waits for them, and re-layouts  11.9 us (27%)
  between operations  0.66 us (2%)
    pallas_call x1, Pallas kernels, device_part(): pl.pallas_call(functools.partial(layer_kernel, docs, parts), out_shape=(j...  31 us
    unnamed x24, local copies, waits for them, and re-layouts  11.9 us

profile of v1, /device:TPU:0, one launch (start us, length us, event | category | flops | bytes accessed | tf_op | source)
XLA Modules:
  0.0 43.5 jit_solution(8238556561328615389)
XLA Ops:
  0.6 0.8 %copy.14.step_ref = f32[1,256,16]{2,1,0:T(8,128)S(1)} copy(f32[1,256,16]{1,2,0:T(8,128)} %param.13) | data formatting | bytes 32768 | tf_op args[2]
  1.4 0.0 copy-start
  1.5 1.6 %copy-done = bf16[1,256,4096]{2,1,0:T(8,128)(2,1)S(1)} copy-done((bf16[1,256,4096]{2,1,0:T(8,128)(2,1)S(1)}, bf16[1,256,4096]{2,1,0:T(8,128)(2,1)}, u32[]{:S(2)}) %copy-start) | copy-done | bytes 2097176
  3.0 0.0 copy-start.1
  3.0 1.0 %copy-done.1 = bf16[1,256,1024]{2,1,0:T(8,128)(2,1)S(1)} copy-done((bf16[1,256,1024]{2,1,0:T(8,128)(2,1)S(1)}, bf16[1,256,1024]{2,1,0:T(8,128)(2,1)}, u32[]{:S(2)}) %copy-start.1) | copy-done | bytes 524312
  4.1 0.0 copy-start.2
  4.1 1.0 %copy-done.2 = bf16[1,256,1024]{2,1,0:T(8,128)(2,1)S(1)} copy-done((bf16[1,256,1024]{2,1,0:T(8,128)(2,1)S(1)}, bf16[1,256,1024]{2,1,0:T(8,128)(2,1)}, u32[]{:S(2)}) %copy-start.2) | copy-done | bytes 524312
  5.1 0.0 copy-start.3
  5.1 0.9 %copy-done.3 = bf16[512,256]{1,0:T(8,128)(2,1)S(1)} copy-done((bf16[512,256]{1,0:T(8,128)(2,1)S(1)}, bf16[512,256]{1,0:T(8,128)(2,1)}, u32[]{:S(2)}) %copy-start.3) | copy-done | bytes 262168
  6.1 0.0 copy-start.4
  6.1 0.9 %copy-done.4 = bf16[4,16,16,128]{3,2,1,0:T(8,128)(2,1)S(1)} copy-done((bf16[4,16,16,128]{3,2,1,0:T(8,128)(2,1)S(1)}, bf16[4,16,16,128]{3,2,1,0:T(8,128)(2,1)}, u32[]{:S(2)}) %copy-start.4) | copy-done | bytes 262168
  7.0 0.0 copy-start.5
  7.0 0.8 %copy-done.5 = bf16[4,3,16,16]{3,2,1,0:T(8,128)(2,1)S(1)} copy-done((bf16[4,3,16,16]{3,2,1,0:T(8,128)(2,1)S(1)}, bf16[4,3,16,16]{3,2,1,0:T(8,128)(2,1)}, u32[]{:S(2)}) %copy-start.5) | copy-done | bytes 6168
  7.8 0.0 copy-start.6
  7.8 0.7 %copy-done.6 = f32[4,1024]{1,0:T(4,128)S(1)} copy-done((f32[4,1024]{1,0:T(4,128)S(1)}, f32[4,1024]{1,0:T(4,128)}, u32[]{:S(2)}) %copy-start.6) | copy-done | bytes 16408
  8.5 0.0 copy-start.7
  8.5 0.7 %copy-done.7 = s32[1,256]{1,0:T(1,128)S(1)} copy-done((s32[1,256]{1,0:T(1,128)S(1)}, s32[1,256]{1,0:T(1,128)}, u32[]{:S(2)}) %copy-start.7) | copy-done | bytes 1048
  9.2 0.0 copy-start.8
  9.2 0.7 %copy-done.8 = s32[4]{0:T(128)S(1)} copy-done((s32[4]{0:T(128)S(1)}, s32[4]{0:T(128)}, u32[]{:S(2)}) %copy-start.8) | copy-done | bytes 40
  9.9 0.0 copy-start.9
  9.9 0.7 %copy-done.9 = f32[16]{0:T(128)S(1)} copy-done((f32[16]{0:T(128)S(1)}, f32[16]{0:T(128)}, u32[]{:S(2)}) %copy-start.9) | copy-done | bytes 88
  10.5 31.0 %shard_map.130 = (f32[128,256]{1,0:T(8,128)S(1)}, bf16[4,16,16,128]{3,2,1,0:T(8,128)(2,1)S(1)}, bf16[4,3,16,16]{3,2,1,0:T(8,128)(2,1)S(1)}) custom-call(s32[4]{0:T(128)S(1)} %copy-done.8, bf16[1,256,4096]{2,1,0:T(8,128)(2,1)S(1)} %copy-done, bf16[1,256,1024]{2,1,0:T(8,128)(2,1)S(1)} %copy-done.1, f32[1,256,16]{2,1,0:T(8,128)S(1)} %copy.14.step_ref, ...), custom_call_target="tpu_custom_call" | custom-call | flops 536870912 | bytes 4194304 | tf_op jit(solution)/shard_map/pallas_call | solution.py:584
  41.5 0.7 %copy.18 = f32[128,256]{1,0:T(8,128)} copy(f32[128,256]{1,0:T(8,128)S(1)} %get-tuple-element.6) | data formatting | bytes 262144
  42.2 0.7 %copy.19 = bf16[4,16,16,128]{3,2,1,0:T(8,128)(2,1)} copy(bf16[4,16,16,128]{3,2,1,0:T(8,128)(2,1)S(1)} %get-tuple-element.7) | data formatting | bytes 524288
  42.9 0.6 %copy.20 = bf16[4,3,16,16]{3,2,1,0:T(8,128)(2,1)} copy(bf16[4,3,16,16]{3,2,1,0:T(8,128)(2,1)S(1)} %get-tuple-element.8) | data formatting | bytes 12288
Async XLA Ops:
  1.4 1.6 %copy-start = (bf16[1,256,4096]{2,1,0:T(8,128)(2,1)S(1)}, bf16[1,256,4096]{2,1,0:T(8,128)(2,1)}, u32[]{:S(2)}) copy-start(bf16[1,256,4096]{2,1,0:T(8,128)(2,1)} %tokens_ref.1) | copy-start | bytes 6291460
  3.0 1.0 %copy-start.1 = (bf16[1,256,1024]{2,1,0:T(8,128)(2,1)S(1)}, bf16[1,256,1024]{2,1,0:T(8,128)(2,1)}, u32[]{:S(2)}) copy-start(bf16[1,256,1024]{2,1,0:T(8,128)(2,1)} %mix_ref.1) | copy-start | bytes 1572868
  4.1 1.0 %copy-start.2 = (bf16[1,256,1024]{2,1,0:T(8,128)(2,1)S(1)}, bf16[1,256,1024]{2,1,0:T(8,128)(2,1)}, u32[]{:S(2)}) copy-start(bf16[1,256,1024]{2,1,0:T(8,128)(2,1)} %grad_ref.1) | copy-start | bytes 1572868
  5.1 0.9 %copy-start.3 = (bf16[512,256]{1,0:T(8,128)(2,1)S(1)}, bf16[512,256]{1,0:T(8,128)(2,1)}, u32[]{:S(2)}) copy-start(bf16[512,256]{1,0:T(8,128)(2,1)} %weight_ref.1) | copy-start | bytes 786436
  6.1 0.9 %copy-start.4 = (bf16[4,16,16,128]{3,2,1,0:T(8,128)(2,1)S(1)}, bf16[4,16,16,128]{3,2,1,0:T(8,128)(2,1)}, u32[]{:S(2)}) copy-start(bf16[4,16,16,128]{3,2,1,0:T(8,128)(2,1)} %state_ref.1) | copy-start | bytes 786436
  7.0 0.8 %copy-start.5 = (bf16[4,3,16,16]{3,2,1,0:T(8,128)(2,1)S(1)}, bf16[4,3,16,16]{3,2,1,0:T(8,128)(2,1)}, u32[]{:S(2)}) copy-start(bf16[4,3,16,16]{3,2,1,0:T(8,128)(2,1)} %conv_ref.1) | copy-start | bytes 18436
  7.8 0.7 %copy-start.6 = (f32[4,1024]{1,0:T(4,128)S(1)}, f32[4,1024]{1,0:T(4,128)}, u32[]{:S(2)}) copy-start(f32[4,1024]{1,0:T(4,128)} %taps_ref.1) | copy-start | bytes 49156
  8.5 0.7 %copy-start.7 = (s32[1,256]{1,0:T(1,128)S(1)}, s32[1,256]{1,0:T(1,128)}, u32[]{:S(2)}) copy-start(s32[1,256]{1,0:T(1,128)} %seg_ref.1) | copy-start | bytes 3076
  9.2 0.7 %copy-start.8 = (s32[4]{0:T(128)S(1)}, s32[4]{0:T(128)}, u32[]{:S(2)}) copy-start(s32[4]{0:T(128)} %carry_ref.1) | copy-start | bytes 52
  9.9 0.7 %copy-start.9 = (f32[16]{0:T(128)S(1)}, f32[16]{0:T(128)}, u32[]{:S(2)}) copy-start(f32[16]{0:T(128)} %param.18) | copy-start | bytes 196

commit v2 on v1

--- a/solution.py
+++ b/solution.py
@@ -203,8 +203,21 @@
 def layer_kernel(
     docs,
     parts,
+    carry_hbm,
+    tokens_hbm,
+    mix_hbm,
+    step_hbm,
+    seg_hbm,
+    grad_hbm,
+    weight_hbm,
+    taps_hbm,
+    rate_hbm,
+    state_hbm,
+    conv_hbm,
+    proj_out,
+    state_out,
+    conv_out,
     carry_ref,
-    tokens_ref,
     mix_ref,
     step_ref,
     seg_ref,
@@ -214,9 +227,6 @@
     rate_ref,
     state_ref,
     conv_ref,
-    proj_out,
-    state_out,
-    conv_out,
     tok_part,
     tok_cols,
     coeff_partial,
@@ -240,8 +250,8 @@
     seg_ext,
     og_scaled,
     val_scaled,
-    first_pre,
-    first_scale,
+    first_step,
+    first_shrink,
     load_sem,
     part_send_sem,
     part_recv_sem,
@@ -250,8 +260,8 @@
 ):
     d = lax.axis_index("doc")
     f = lax.axis_index("fsdp")
-    length, channels = mix_ref.shape[1], mix_ref.shape[2]
-    heads = step_ref.shape[2]
+    length, channels = mix_ref.shape
+    heads = step_ref.shape[0]
     head_dim = channels // heads
     part_p = head_dim // docs
     width = weight_ref.shape[1]
@@ -262,23 +272,28 @@
     out_rows = proj_out.shape[0]
     taps = taps_ref.shape[0]
 
+    own_columns = pl.ds(pl.multiple_of(f * depth, 128), depth)
+    pairs = [
+        (carry_hbm, carry_ref),
+        (state_hbm, state_ref),
+        (conv_hbm, conv_ref),
+        (tokens_hbm.at[0, :, own_columns], tok_part),
+        (weight_hbm, weight_ref),
+        (step_hbm.at[0], step_ref),
+        (rate_hbm, rate_ref),
+        (seg_hbm, seg_ref),
+        (taps_hbm, taps_ref),
+        (mix_hbm.at[0], mix_ref),
+        (grad_hbm.at[0], grad_ref),
+    ]
+    for q in range(docs):
+        columns = pl.ds(pl.multiple_of((q * parts + f) * out_rows, 128), out_rows)
+        pairs.append(
+            (tokens_hbm.at[0, :, columns], tok_cols.at[:, pl.ds(q * out_rows, out_rows)])
+        )
     loads = [
-        pltpu.make_async_copy(
-            tokens_ref.at[0, :, pl.ds(pl.multiple_of(f * depth, 128), depth)],
-            tok_part,
-            load_sem.at[0],
-        )
-    ]
-    for q in range(docs):
-        loads.append(
-            pltpu.make_async_copy(
-                tokens_ref.at[
-                    0, :, pl.ds(pl.multiple_of((q * parts + f) * out_rows, 128), out_rows)
-                ],
-                tok_cols.at[:, pl.ds(q * out_rows, out_rows)],
-                load_sem.at[1 + q],
-            )
-        )
+        pltpu.make_async_copy(src, dst, load_sem.at[i]) for i, (src, dst) in enumerate(pairs)
+    ]
     for load in loads:
         load.start()
 
@@ -315,6 +330,8 @@
     def rows_of(owner):
         return pl.ds(pl.multiple_of(owner * block, block), block)
 
+    for load in loads[:3]:
+        load.wait()
     for r in range(slots):
         source = carry_ref[r]
         usable = jnp.where(source >= 0, 1.0, 0.0)
@@ -322,7 +339,8 @@
         state_send[r] = (state_ref[index].astype(F32) * usable).astype(BF16)
         conv_send[r] = (conv_ref[index].astype(F32) * usable).astype(BF16)
 
-    loads[0].wait()
+    for load in loads[3:5]:
+        load.wait()
     coeff_partial[...] = dot_nn(tok_part[...], weight_ref[...])
 
     pl.semaphore_wait(barrier, parts - 1 + docs - 1)
@@ -343,10 +361,21 @@
     conv_recv[d] = conv_send[d]
     state_recv[:, d] = state_send[d]
 
+    for load in loads[5:11]:
+        load.wait()
     lower = iota((length, length), 0) >= iota((length, length), 1)
-    steps = step_ref[0]
-    log_decay = dot_nn(
-        jnp.where(lower, 1.0, 0.0), -(rate_ref[...] * steps), precision=lax.Precision.HIGHEST
+    rate = jnp.sum(
+        jnp.where(iota((heads, heads), 0) == iota((heads, heads), 1), rate_ref[...], 0.0),
+        axis=1,
+        keepdims=True,
+    )
+    steps = step_ref[...]
+    log_decay = lax.dot_general(
+        -(rate * steps),
+        jnp.where(lower, 1.0, 0.0),
+        (((1,), (1,)), ((), ())),
+        precision=lax.Precision.HIGHEST,
+        preferred_element_type=F32,
     )
 
     def halves(x):
@@ -361,33 +390,40 @@
     seg_cols = jnp.broadcast_to(seg_row, (128, length)).T
     seg_ext[8:, :] = seg_cols
     seg_ext[:8, :] = jnp.broadcast_to(seg_cols[:1], (8, 128))
-    allowed = lower & (seg_cols[:, :1] == seg_row)
     opening = seg_cols == seg_cols[:1]
 
-    for copy in conv_copies:
-        copy.wait_recv()
-
-    def place(q):
-        lane = iota((part_p, channels), 1)
-        return jnp.where(
-            lax.rem(lane, head_dim) == iota((part_p, channels), 0) + q * part_p, 1.0, 0.0
+    def scaled_values(preact, step, shrink_factor):
+        mixed = (preact / (1.0 + jnp.exp(-preact))).astype(BF16).astype(F32)
+        values = (step * mixed).astype(BF16).astype(F32)
+        return (values * shrink_factor).astype(BF16)
+
+    ext[:8, :] = jnp.zeros((8, channels), F32)
+
+    def chunk(c, carry):
+        lanes = pl.ds(pl.multiple_of(c * 128, 128), 128)
+        expand = jnp.where(
+            iota((heads, 128), 0) == lax.div(iota((heads, 128), 1) + c * 128, head_dim), 1.0, 0.0
         ).astype(BF16)
 
-    places = [place(q) for q in range(docs)]
-    head_rows = (taps - 1) * heads
-    own_head = (
-        lax.div(iota((taps - 1, heads, channels), 2), head_dim)
-        == iota((taps - 1, heads, channels), 1)
-    )
-    spread = jnp.zeros((head_rows, channels), F32)
-    for q in range(docs):
-        spread = spread + dot_nn(conv_recv[q].reshape(head_rows, part_p), places[q])
-    carried_rows = jnp.sum(
-        jnp.where(own_head, spread.reshape(taps - 1, heads, channels), 0.0), axis=1
-    )
-    ext[:8, :] = jnp.zeros((8, channels), F32)
-    ext[8 - (taps - 1) : 8, :] = carried_rows
-    ext[8:, :] = mix_ref[0].astype(F32)
+        def per_channel(pair):
+            return dot_tn(pair[0], expand) + dot_tn(pair[1], expand)
+
+        ext[8:, lanes] = mix_ref[:, lanes].astype(F32)
+        preact = jnp.zeros((length, 128), F32)
+        for k in range(taps):
+            same = seg_ext[8 - k : 8 - k + length, :] == seg_cols
+            window = ext[8 - k : 8 - k + length, lanes]
+            preact = preact + jnp.where(same, taps_ref[k : k + 1, lanes] * window, 0.0)
+        step_c = per_channel(step_halves)
+        shrink_c = per_channel(shrink)
+        val_scaled[:, lanes] = scaled_values(preact, step_c, shrink_c)
+        og_scaled[:, lanes] = (grad_ref[:, lanes].astype(F32) * per_channel(grow)).astype(BF16)
+        first_step[:, lanes] = step_c[:16]
+        first_shrink[:, lanes] = shrink_c[:16]
+        return carry
+
+    chunks = channels // 128
+    lax.fori_loop(0, chunks // 2, chunk, 0)
 
     for copy in coeff_copies:
         copy.wait_recv()
@@ -401,32 +437,45 @@
     for copy in gather_copies:
         copy.start()
 
-    def chunk(c, carry):
-        lanes = pl.ds(pl.multiple_of(c * 128, 128), 128)
-        expand = jnp.where(
-            iota((heads, 128), 0) == lax.div(iota((heads, 128), 1) + c * 128, head_dim), 1.0, 0.0
+    lax.fori_loop(chunks // 2, chunks, chunk, 0)
+
+    for copy in conv_copies:
+        copy.wait_recv()
+
+    def place(q):
+        lane = iota((part_p, channels), 1)
+        return jnp.where(
+            lax.rem(lane, head_dim) == iota((part_p, channels), 0) + q * part_p, 1.0, 0.0
         ).astype(BF16)
 
-        def per_channel(pair):
-            return dot_nn(pair[0], expand) + dot_nn(pair[1], expand)
-
-        preact = jnp.zeros((length, 128), F32)
-        for k in range(taps):
-            same = seg_ext[8 - k : 8 - k + length, :] == seg_cols
-            window = ext[8 - k : 8 - k + length, lanes]
-            preact = preact + jnp.where(same, taps_ref[k : k + 1, lanes] * window, 0.0)
-        step_c = per_channel(step_halves)
-        shrink_c = per_channel(shrink)
-        mixed = (preact / (1.0 + jnp.exp(-preact))).astype(BF16).astype(F32)
-        values = (step_c * mixed).astype(BF16).astype(F32)
-        val_scaled[:, lanes] = (values * shrink_c).astype(BF16)
-        og_scaled[:, lanes] = (grad_ref[0, :, lanes].astype(F32) * per_channel(grow)).astype(BF16)
-        first_pre[:, lanes] = preact[:8]
-        first_scale[:, lanes] = (step_c * shrink_c)[:8]
-        return carry
-
-    lax.fori_loop(0, channels // 128, chunk, 0)
-    score_grad = jnp.where(allowed, dot_nt(og_scaled[...], val_scaled[...]), 0.0).astype(BF16)
+    places = [place(q) for q in range(docs)]
+    head_rows = (taps - 1) * heads
+    own_head = (
+        lax.div(iota((taps - 1, heads, channels), 2), head_dim)
+        == iota((taps - 1, heads, channels), 1)
+    )
+    spread = jnp.zeros((head_rows, channels), F32)
+    for q in range(docs):
+        spread = spread + dot_nn(conv_recv[q].reshape(head_rows, part_p), places[q])
+    carried_rows = jnp.sum(
+        jnp.where(own_head, spread.reshape(taps - 1, heads, channels), 0.0), axis=1
+    )
+    ext[8 - (taps - 1) : 8, :] = carried_rows
+    pre = jnp.zeros((16, channels), F32)
+    for k in range(taps):
+        same = seg_ext[8 - k : 24 - k, :1] == seg_cols[:16, :1]
+        window = ext[8 - k : 24 - k, :]
+        pre = pre + jnp.where(same, taps_ref[k : k + 1, :] * window, 0.0)
+    val_scaled[:16, :] = scaled_values(pre, first_step[...], first_shrink[...])
+
+    upper = iota((length, length), 0) <= iota((length, length), 1)
+    same_doc = seg_cols[:, :1] == seg_row
+    score_grad = jnp.where(
+        lower & same_doc, dot_nt(og_scaled[...], val_scaled[...]), 0.0
+    ).astype(BF16)
+    score_grad_t = jnp.where(
+        upper & same_doc, dot_nt(val_scaled[...], og_scaled[...]), 0.0
+    ).astype(BF16)
 
     for copy in state_copies:
         copy.wait_recv()
@@ -438,7 +487,7 @@
         copy.wait_recv()
     write_coeff = coeff[:, :nstate]
     read_coeff = coeff[:, nstate:]
-    cg_partial[:, :nstate] = dot_tn(score_grad, read_coeff)
+    cg_partial[:, :nstate] = dot_nn(score_grad_t, read_coeff)
     cg_partial[:, nstate:] = dot_nn(score_grad, write_coeff) + from_state
     sum_copies = [
         part_copy(2, j, cg_partial.at[rows_of(lax.rem(f + j, parts))], cg_recv.at[j])
@@ -462,9 +511,9 @@
     first_allowed = first_seg & (iota((16, length), 1) >= iota((16, length), 0))
     first_scores = jnp.where(first_allowed, first_scores, 0.0).astype(BF16)
     first_grad = dot_nn(first_scores, og_scaled[...])[:8]
-    pre = first_pre[...]
+    pre = pre[:8]
     gate = 1.0 / (1.0 + jnp.exp(-pre))
-    pre_grad = first_grad * first_scale[...] * gate * (1.0 + pre * (1.0 - gate))
+    pre_grad = first_grad * first_step[:8] * first_shrink[:8] * gate * (1.0 + pre * (1.0 - gate))
     pre_grad = jnp.where(seg_cols[:8, :1] == seg_cols[:1, :1], pre_grad, 0.0)
     conv_rows = []
     for row in range(taps - 1):
@@ -496,7 +545,7 @@
     cg_copies = [part_copy(3, j, cg.at[rows_of(f)], cg.at[rows_of(f)]) for j in range(1, parts)]
     for copy in cg_copies:
         copy.start()
-    for load in loads[1:]:
+    for load in loads[11:]:
         load.wait()
 
     for copy in cg_copies:
@@ -588,13 +637,19 @@
             jax.ShapeDtypeStruct(carried_state.shape, BF16),
             jax.ShapeDtypeStruct(carried_conv.shape, BF16),
         ),
-        in_specs=[
-            pl.BlockSpec(memory_space=pltpu.SMEM),
-            pl.BlockSpec(memory_space=pl.ANY),
-        ]
-        + [vmem] * 9,
+        in_specs=[pl.BlockSpec(memory_space=pltpu.HBM)] * 11,
         out_specs=(vmem, vmem, vmem),
         scratch_shapes=[
+            pltpu.SMEM(carry_from.shape, jnp.int32),
+            pltpu.VMEM((length, channels), BF16),
+            pltpu.VMEM((heads, length), F32),
+            pltpu.VMEM(doc_ids.shape, jnp.int32),
+            pltpu.VMEM((length, channels), BF16),
+            pltpu.VMEM(proj_weight.shape, BF16),
+            pltpu.VMEM(conv_weight.shape, F32),
+            pltpu.VMEM((1, heads), F32),
+            pltpu.VMEM(carried_state.shape, BF16),
+            pltpu.VMEM(carried_conv.shape, BF16),
             pltpu.VMEM((length, depth), BF16),
             pltpu.VMEM((length, docs * out_rows), BF16),
             pltpu.VMEM((length, width), F32),
@@ -618,16 +673,16 @@
             pltpu.VMEM((length + 8, 128), F32),
             pltpu.VMEM((length, channels), BF16),
             pltpu.VMEM((length, channels), BF16),
-            pltpu.VMEM((8, channels), F32),
-            pltpu.VMEM((8, channels), F32),
-            pltpu.SemaphoreType.DMA((1 + docs,)),
+            pltpu.VMEM((16, channels), F32),
+            pltpu.VMEM((16, channels), F32),
+            pltpu.SemaphoreType.DMA((11 + docs,)),
             pltpu.SemaphoreType.DMA((4, parts)),
             pltpu.SemaphoreType.DMA((4, parts)),
             pltpu.SemaphoreType.DMA((5, docs)),
             pltpu.SemaphoreType.DMA((5, docs)),
         ],
         compiler_params=pltpu.CompilerParams(
-            collective_id=0, has_side_effects=True, vmem_limit_bytes=40 * 1024 * 1024
+            collective_id=0, has_side_effects=True, vmem_limit_bytes=60 * 1024 * 1024
         ),
         cost_estimate=pl.CostEstimate(
             flops=2 * length * channels * length * 4, bytes_accessed=4 << 20, transcendentals=0
@@ -636,7 +691,7 @@
         carry_from,
         tokens_in,
         mix_in,
-        step_size,
+        jnp.swapaxes(step_size, 1, 2),
         doc_ids,
         out_grad,
         proj_weight,

time: 44 us -> 36.7 us (0.83)
  local copies, waits for them, and re-layouts: 11.9 us -> 4.66 us
    unnamed x24 -> x3, local copies, waits for them, and re-layouts: 11.9 us -> 4.66 us
where the time goes in v2:
time: 36.7 us; the launch traced here: 36.5 us
  Pallas kernels  31.2 us (85%)
  local copies, waits for them, and re-layouts  4.66 us (13%)
  between operations  0.64 us (2%)
    pallas_call x1, Pallas kernels, device_part(): pl.pallas_call(functools.partial(layer_kernel, docs, parts), out_shape=(j...  31.2 us
    unnamed x3, local copies, waits for them, and re-layouts  4.66 us

profile of v2, /device:TPU:0, one launch (start us, length us, event | category | flops | bytes accessed | tf_op | source)
XLA Modules:
  0.0 36.5 jit_solution(8636978169471161185)
XLA Ops:
  0.6 31.2 %shard_map.130 = (f32[128,256]{1,0:T(8,128)}, bf16[4,16,16,128]{3,2,1,0:T(8,128)(2,1)}, bf16[4,3,16,16]{3,2,1,0:T(8,128)(2,1)}) custom-call(s32[4]{0:T(128)} %carry_hbm.1, bf16[1,256,4096]{2,1,0:T(8,128)(2,1)} %tokens_hbm.1, bf16[1,256,1024]{2,1,0:T(8,128)(2,1)} %mix_hbm.1, f32[1,16,256]{2,1,0:T(8,128)} %bitcast.2, s32[1,256]{1,0:T(1,128)} %seg_hbm.1, ...), custom_call_target="tpu_custom_call" | custom-call | flops 536870912 | bytes 4194304 | tf_op jit(solution)/shard_map/pallas_call | solution.py:633
  31.8 1.6 %copy.17 = f32[128,256]{1,0:T(8,128)} copy(f32[128,256]{1,0:T(8,128)} %get-tuple-element.6) | data formatting | bytes 262144
  33.4 1.7 %copy.18 = bf16[4,16,16,128]{3,2,1,0:T(8,128)(2,1)} copy(bf16[4,16,16,128]{3,2,1,0:T(8,128)(2,1)} %get-tuple-element.7) | data formatting | bytes 524288
  35.1 1.4 %copy.19 = bf16[4,3,16,16]{3,2,1,0:T(8,128)(2,1)} copy(bf16[4,3,16,16]{3,2,1,0:T(8,128)(2,1)} %get-tuple-element.8) | data formatting | bytes 12288

commit v3 on v2

--- a/solution.py
+++ b/solution.py
@@ -214,9 +214,10 @@
     rate_hbm,
     state_hbm,
     conv_hbm,
-    proj_out,
-    state_out,
-    conv_out,
+    fin_own,
+    fin_recv,
+    sgrad_recv,
+    cgrad_recv,
     carry_ref,
     mix_ref,
     step_ref,
@@ -233,6 +234,7 @@
     coeff_recv,
     coeff,
     cg_partial,
+    cg_send,
     cg_recv,
     cg,
     state_send,
@@ -240,12 +242,9 @@
     conv_send,
     conv_recv,
     sgrad_send,
-    sgrad_recv,
     cgrad_send,
-    cgrad_recv,
-    fin_own,
+    fin_part,
     fin_send,
-    fin_recv,
     ext,
     seg_ext,
     og_scaled,
@@ -253,6 +252,7 @@
     first_step,
     first_shrink,
     load_sem,
+    store_sem,
     part_send_sem,
     part_recv_sem,
     doc_send_sem,
@@ -269,7 +269,7 @@
     slots = state_ref.shape[0]
     depth = weight_ref.shape[0]
     block = length // parts
-    out_rows = proj_out.shape[0]
+    out_rows = fin_own.shape[0]
     taps = taps_ref.shape[0]
 
     own_columns = pl.ds(pl.multiple_of(f * depth, 128), depth)
@@ -330,6 +330,21 @@
     def rows_of(owner):
         return pl.ds(pl.multiple_of(owner * block, block), block)
 
+    lane = iota((1, channels), 1)
+    head_of_lane = lax.div(lane, head_dim)
+    lane_in_head = lane - head_of_lane * head_dim
+    places = [
+        jnp.where(
+            jnp.broadcast_to(lane_in_head, (part_p, channels))
+            == iota((part_p, channels), 0) + q * part_p,
+            1.0,
+            0.0,
+        ).astype(BF16)
+        for q in range(docs)
+    ]
+    head_rows = (taps - 1) * heads
+    own_head = jnp.broadcast_to(head_of_lane, (heads, channels)) == iota((heads, channels), 0)
+
     for load in loads[:3]:
         load.wait()
     for r in range(slots):
@@ -379,8 +394,9 @@
     )
 
     def halves(x):
-        top = x.astype(BF16)
-        return top, (x - top.astype(F32)).astype(BF16)
+        top = x.astype(BF16).astype(F32)
+        both = jnp.concatenate([top, x - top, jnp.zeros((128 - 2 * heads, length), F32)], axis=0)
+        return both.T.astype(BF16)
 
     grow = halves(jnp.exp(log_decay))
     shrink = halves(jnp.exp(-log_decay))
@@ -401,12 +417,14 @@
 
     def chunk(c, carry):
         lanes = pl.ds(pl.multiple_of(c * 128, 128), 128)
-        expand = jnp.where(
-            iota((heads, 128), 0) == lax.div(iota((heads, 128), 1) + c * 128, head_dim), 1.0, 0.0
-        ).astype(BF16)
-
-        def per_channel(pair):
-            return dot_tn(pair[0], expand) + dot_tn(pair[1], expand)
+        row = iota((128, 128), 0)
+        head = jnp.broadcast_to(
+            lax.div(iota((1, 128), 1) + c * 128, head_dim), (128, 128)
+        )
+        expand = jnp.where((row == head) | (row == head + heads), 1.0, 0.0).astype(BF16)
+
+        def per_channel(both):
+            return dot_nn(both, expand)
 
         ext[8:, lanes] = mix_ref[:, lanes].astype(F32)
         preact = jnp.zeros((length, 128), F32)
@@ -442,23 +460,11 @@
     for copy in conv_copies:
         copy.wait_recv()
 
-    def place(q):
-        lane = iota((part_p, channels), 1)
-        return jnp.where(
-            lax.rem(lane, head_dim) == iota((part_p, channels), 0) + q * part_p, 1.0, 0.0
-        ).astype(BF16)
-
-    places = [place(q) for q in range(docs)]
-    head_rows = (taps - 1) * heads
-    own_head = (
-        lax.div(iota((taps - 1, heads, channels), 2), head_dim)
-        == iota((taps - 1, heads, channels), 1)
-    )
     spread = jnp.zeros((head_rows, channels), F32)
     for q in range(docs):
         spread = spread + dot_nn(conv_recv[q].reshape(head_rows, part_p), places[q])
     carried_rows = jnp.sum(
-        jnp.where(own_head, spread.reshape(taps - 1, heads, channels), 0.0), axis=1
+        jnp.where(own_head[None], spread.reshape(taps - 1, heads, channels), 0.0), axis=1
     )
     ext[8 - (taps - 1) : 8, :] = carried_rows
     pre = jnp.zeros((16, channels), F32)
@@ -489,8 +495,9 @@
     read_coeff = coeff[:, nstate:]
     cg_partial[:, :nstate] = dot_nn(score_grad_t, read_coeff)
     cg_partial[:, nstate:] = dot_nn(score_grad, write_coeff) + from_state
+    cg_send[...] = cg_partial[...].astype(BF16)
     sum_copies = [
-        part_copy(2, j, cg_partial.at[rows_of(lax.rem(f + j, parts))], cg_recv.at[j])
+        part_copy(2, j, cg_send.at[rows_of(lax.rem(f + j, parts))], cg_recv.at[j])
         for j in range(1, parts)
     ]
     for copy in sum_copies:
@@ -522,7 +529,7 @@
             position = row - (taps - 1) + k
             running = running + taps_ref[k : k + 1, :] * pre_grad[position : position + 1]
         conv_rows.append(
-            jnp.where(own_head[0], jnp.broadcast_to(running, (heads, channels)), 0.0).astype(BF16)
+            jnp.where(own_head, jnp.broadcast_to(running, (heads, channels)), 0.0).astype(BF16)
         )
     for q in range(docs):
         for row in range(taps - 1):
@@ -533,50 +540,43 @@
     ]
     for copy in cgrad_copies:
         copy.start()
-    sgrad_recv[d] = sgrad_send[:, d]
-    cgrad_recv[d] = cgrad_send[d]
+    stores = [
+        pltpu.make_async_copy(sgrad_send.at[:, d], sgrad_recv.at[d], store_sem.at[0]),
+        pltpu.make_async_copy(cgrad_send.at[d], cgrad_recv.at[d], store_sem.at[1]),
+    ]
+    for store in stores:
+        store.start()
+    for load in loads[11:]:
+        load.wait()
+    tok_rows = tok_cols[...].T
 
     for copy in sum_copies:
         copy.wait_recv()
     total = cg_partial[rows_of(f)]
     for j in range(1, parts):
-        total = total + cg_recv[j]
+        total = total + cg_recv[j].astype(F32)
     cg[rows_of(f)] = total.astype(BF16)
     cg_copies = [part_copy(3, j, cg.at[rows_of(f)], cg.at[rows_of(f)]) for j in range(1, parts)]
     for copy in cg_copies:
         copy.start()
-    for load in loads[11:]:
-        load.wait()
 
     for copy in cg_copies:
         copy.wait_recv()
-    product = dot_tn(tok_cols[...], cg[...])
-    fin_own[...] = product.reshape(docs, out_rows, width)
-    fin_send[...] = product.astype(BF16).reshape(docs, out_rows, width)
+    product = dot_nn(tok_rows, cg[...]).reshape(docs, out_rows, width)
+    fin_send[...] = product.astype(BF16)
     fin_copies = [
-        doc_copy(4, j, fin_send.at[lax.rem(d + j, docs)], fin_recv.at[j]) for j in range(1, docs)
+        doc_copy(4, j, fin_send.at[lax.rem(d + j, docs)], fin_recv.at[j - 1])
+        for j in range(1, docs)
     ]
     for copy in fin_copies:
         copy.start()
-
-    for copy in sgrad_copies + cgrad_copies:
+    fin_part[...] = product
+    stores.append(pltpu.make_async_copy(fin_part.at[d], fin_own, store_sem.at[2]))
+    stores[2].start()
+    for copy in sgrad_copies + cgrad_copies + fin_copies:
         copy.wait_recv()
-    for s in range(slots):
-        row_of = jnp.int32(0)
-        found = jnp.float32(0.0)
-        for r in range(slots):
-            hit = carry_ref[r] == s
-            row_of = jnp.where(hit, r, row_of)
-            found = jnp.where(hit, 1.0, found)
-        state_out[s] = (sgrad_recv[row_of].astype(F32) * found).astype(BF16)
-        conv_out[s] = (cgrad_recv[row_of].astype(F32) * found).astype(BF16)
-
-    for copy in fin_copies:
-        copy.wait_recv()
-    result = fin_own[d]
-    for j in range(1, docs):
-        result = result + fin_recv[j].astype(F32)
-    proj_out[...] = result
+    for store in stores:
+        store.wait()
 
     for copies in (
         conv_copies,
@@ -591,6 +591,52 @@
     ):
         for copy in copies:
             copy.wait_send()
+
+
+def finish_kernel(
+    carry_hbm,
+    own_hbm,
+    recv_hbm,
+    sgrad_hbm,
+    cgrad_hbm,
+    proj_out,
+    state_out,
+    conv_out,
+    carry_ref,
+    own_ref,
+    recv_ref,
+    sgrad_ref,
+    cgrad_ref,
+    load_sem,
+):
+    pairs = (
+        (carry_hbm, carry_ref),
+        (sgrad_hbm, sgrad_ref),
+        (cgrad_hbm, cgrad_ref),
+        (own_hbm, own_ref),
+        (recv_hbm, recv_ref),
+    )
+    loads = [
+        pltpu.make_async_copy(src, dst, load_sem.at[i]) for i, (src, dst) in enumerate(pairs)
+    ]
+    for load in loads:
+        load.start()
+    for load in loads:
+        load.wait()
+    slots = state_out.shape[0]
+    for s in range(slots):
+        row_of = jnp.int32(0)
+        found = jnp.float32(0.0)
+        for r in range(slots):
+            hit = carry_ref[r] == s
+            row_of = jnp.where(hit, r, row_of)
+            found = jnp.where(hit, 1.0, found)
+        state_out[s] = (sgrad_ref[row_of].astype(F32) * found).astype(BF16)
+        conv_out[s] = (cgrad_ref[row_of].astype(F32) * found).astype(BF16)
+    result = own_ref[...]
+    for j in range(recv_ref.shape[0]):
+        result = result + recv_ref[j].astype(F32)
+    proj_out[...] = result
 
 
 def device_part(docs, parts, *args):
@@ -620,6 +666,7 @@
         and slots == docs
         and part_p % 16 == 0
         and heads % 16 == 0
+        and 2 * heads <= 128
         and block % 16 == 0
         and out_rows % 128 == 0
         and depth % 128 == 0
@@ -630,15 +677,18 @@
     if not aligned:
         return shards(*args)
     vmem = pl.BlockSpec(memory_space=pltpu.VMEM)
-    return pl.pallas_call(
+    hbm = pl.BlockSpec(memory_space=pltpu.HBM)
+    landed = (
+        jax.ShapeDtypeStruct((out_rows, width), F32),
+        jax.ShapeDtypeStruct((docs - 1, out_rows, width), BF16),
+        jax.ShapeDtypeStruct(carried_state.shape, BF16),
+        jax.ShapeDtypeStruct(carried_conv.shape, BF16),
+    )
+    buffers = pl.pallas_call(
         functools.partial(layer_kernel, docs, parts),
-        out_shape=(
-            jax.ShapeDtypeStruct((out_rows, width), F32),
-            jax.ShapeDtypeStruct(carried_state.shape, BF16),
-            jax.ShapeDtypeStruct(carried_conv.shape, BF16),
-        ),
-        in_specs=[pl.BlockSpec(memory_space=pltpu.HBM)] * 11,
-        out_specs=(vmem, vmem, vmem),
+        out_shape=landed,
+        in_specs=[hbm] * 11,
+        out_specs=(hbm,) * 4,
         scratch_shapes=[
             pltpu.SMEM(carry_from.shape, jnp.int32),
             pltpu.VMEM((length, channels), BF16),
@@ -656,18 +706,16 @@
             pltpu.VMEM((parts, block, width), F32),
             pltpu.VMEM((length, width), BF16),
             pltpu.VMEM((length, width), F32),
-            pltpu.VMEM((parts, block, width), F32),
+            pltpu.VMEM((length, width), BF16),
+            pltpu.VMEM((parts, block, width), BF16),
             pltpu.VMEM((length, width), BF16),
             pltpu.VMEM((slots, heads, part_p, nstate), BF16),
             pltpu.VMEM((heads, docs, part_p, nstate), BF16),
             pltpu.VMEM((slots, taps - 1, heads, part_p), BF16),
             pltpu.VMEM((docs, taps - 1, heads, part_p), BF16),
             pltpu.VMEM((heads, docs, part_p, nstate), BF16),
-            pltpu.VMEM((docs, heads, part_p, nstate), BF16),
-            pltpu.VMEM((docs, taps - 1, heads, part_p), BF16),
             pltpu.VMEM((docs, taps - 1, heads, part_p), BF16),
             pltpu.VMEM((docs, out_rows, width), F32),
-            pltpu.VMEM((docs, out_rows, width), BF16),
             pltpu.VMEM((docs, out_rows, width), BF16),
             pltpu.VMEM((length + 8, channels), F32),
             pltpu.VMEM((length + 8, 128), F32),
@@ -676,6 +724,7 @@
             pltpu.VMEM((16, channels), F32),
             pltpu.VMEM((16, channels), F32),
             pltpu.SemaphoreType.DMA((11 + docs,)),
+            pltpu.SemaphoreType.DMA((3,)),
             pltpu.SemaphoreType.DMA((4, parts)),
             pltpu.SemaphoreType.DMA((4, parts)),
             pltpu.SemaphoreType.DMA((5, docs)),
@@ -700,6 +749,20 @@
         carried_state,
         carried_conv,
     )
+    return pl.pallas_call(
+        finish_kernel,
+        out_shape=(
+            jax.ShapeDtypeStruct((out_rows, width), F32),
+            jax.ShapeDtypeStruct(carried_state.shape, BF16),
+            jax.ShapeDtypeStruct(carried_conv.shape, BF16),
+        ),
+        in_specs=[hbm] * 5,
+        out_specs=(vmem,) * 3,
+        scratch_shapes=[pltpu.SMEM(carry_from.shape, jnp.int32)]
+        + [pltpu.VMEM(leaf.shape, leaf.dtype) for leaf in landed]
+        + [pltpu.SemaphoreType.DMA((5,))],
+        compiler_params=pltpu.CompilerParams(vmem_limit_bytes=60 * 1024 * 1024),
+    )(carry_from, *buffers)
 
 
 def solution(mesh):

time: 36.7 us -> 31.9 us (0.87)
  local copies, waits for them, and re-layouts: 4.66 us -> 0 us
    unnamed x3 -> x0, local copies, waits for them, and re-layouts: 4.66 us -> none
    pallas_call x1 -> x2, Pallas kernels: 31.2 us -> 31.1 us  [the longest x1 29.1 us: device_part(): pl.pallas_call(functools.partial(layer_kernel, docs, parts), out_shape=la...]
where the time goes in v3:
time: 31.9 us; the launch traced here: 31.7 us
  Pallas kernels  31.1 us (97%)
  between operations  0.64 us (2%)
    pallas_call x1, Pallas kernels, device_part(): pl.pallas_call(functools.partial(layer_kernel, docs, parts), out_shape=la...  29.1 us
    pallas_call x1, Pallas kernels, device_part(): pl.pallas_call(finish_kernel, out_shape=(jax.ShapeDtypeStruct((out_rows,...  1.95 us

profile of v3, /device:TPU:0, one launch (start us, length us, event | category | flops | bytes accessed | tf_op | source)
XLA Modules:
  0.0 31.7 jit_solution(10581977334917355268)
XLA Ops:
  0.6 29.1 %shard_map.130 = (f32[128,256]{1,0:T(8,128)}, bf16[3,128,256]{2,1,0:T(8,128)(2,1)}, bf16[4,16,16,128]{3,2,1,0:T(8,128)(2,1)}, bf16[4,3,16,16]{3,2,1,0:T(8,128)(2,1)}) custom-call(s32[4]{0:T(128)} %carry_hbm.3, bf16[1,256,4096]{2,1,0:T(8,128)(2,1)} %tokens_hbm.1, bf16[1,256,1024]{2,1,0:T(8,128)(2,1)} %mix_hbm.1, f32[1,16,256]{2,1,0:T(8,128)} %bitcast.2, ...), custom_call_target="tpu_custom_call" | custom-call | flops 536870912 | bytes 4194304 | tf_op jit(solution)/shard_map/pallas_call | solution.py:687
  29.8 2.0 %shard_map.131 = (f32[128,256]{1,0:T(8,128)}, bf16[4,16,16,128]{3,2,1,0:T(8,128)(2,1)}, bf16[4,3,16,16]{3,2,1,0:T(8,128)(2,1)}) custom-call(s32[4]{0:T(128)} %carry_hbm.3, f32[128,256]{1,0:T(8,128)} %get-tuple-element.7.own_hbm, bf16[3,128,256]{2,1,0:T(8,128)(2,1)} %get-tuple-element.8.recv_hbm, bf16[4,16,16,128]{3,2,1,0:T(8,128)(2,1)} %get-tuple-element.9.sgrad_hbm, ...), custom_call_target="tpu_custom_call" | custom-call | tf_op jit(solution)/shard_map/pallas_call | solution.py:752

commit v4 on v3

--- a/solution.py
+++ b/solution.py
@@ -231,6 +231,7 @@
     tok_part,
     tok_cols,
     coeff_partial,
+    coeff_send,
     coeff_recv,
     coeff,
     cg_partial,
@@ -357,6 +358,7 @@
     for load in loads[3:5]:
         load.wait()
     coeff_partial[...] = dot_nn(tok_part[...], weight_ref[...])
+    coeff_send[...] = coeff_partial[...].astype(BF16)
 
     pl.semaphore_wait(barrier, parts - 1 + docs - 1)
 
@@ -364,7 +366,7 @@
         doc_copy(0, j, conv_send.at[lax.rem(d + j, docs)], conv_recv.at[d]) for j in range(1, docs)
     ]
     coeff_copies = [
-        part_copy(0, j, coeff_partial.at[rows_of(lax.rem(f + j, parts))], coeff_recv.at[j])
+        part_copy(0, j, coeff_send.at[rows_of(lax.rem(f + j, parts))], coeff_recv.at[j])
         for j in range(1, parts)
     ]
     state_copies = [
@@ -447,7 +449,7 @@
         copy.wait_recv()
     total = coeff_partial[rows_of(f)]
     for j in range(1, parts):
-        total = total + coeff_recv[j]
+        total = total + coeff_recv[j].astype(F32)
     coeff[rows_of(f)] = total.astype(BF16)
     gather_copies = [
         part_copy(1, j, coeff.at[rows_of(f)], coeff.at[rows_of(f)]) for j in range(1, parts)
@@ -456,6 +458,21 @@
         copy.start()
 
     lax.fori_loop(chunks // 2, chunks, chunk, 0)
+
+    for copy in gather_copies:
+        copy.wait_recv()
+    write_coeff = coeff[:, :nstate]
+    read_coeff = coeff[:, nstate:]
+    open_read = jnp.where(opening, read_coeff.astype(F32), 0.0).astype(BF16)
+    sgrad_send[...] = (
+        dot_tn(og_scaled[...], open_read).astype(BF16).reshape(heads, docs, part_p, nstate)
+    )
+    sgrad_copies = [
+        doc_copy(2, j, sgrad_send.at[:, lax.rem(d + j, docs)], sgrad_recv.at[d])
+        for j in range(1, docs)
+    ]
+    for copy in sgrad_copies:
+        copy.start()
 
     for copy in conv_copies:
         copy.wait_recv()
@@ -483,36 +500,31 @@
         upper & same_doc, dot_nt(val_scaled[...], og_scaled[...]), 0.0
     ).astype(BF16)
 
+    halves_of = [pl.ds(0, nstate), pl.ds(nstate, nstate)]
+    sum_copies = [[], []]
+
+    def send_half(half, value):
+        columns = halves_of[half]
+        cg_partial[:, columns] = value
+        cg_send[:, columns] = value.astype(BF16)
+        for j in range(1, parts):
+            copy = part_copy(
+                2 + half,
+                j,
+                cg_send.at[rows_of(lax.rem(f + j, parts)), columns],
+                cg_recv.at[j, :, columns],
+            )
+            copy.start()
+            sum_copies[half].append(copy)
+
+    send_half(0, dot_nn(score_grad_t, read_coeff))
     for copy in state_copies:
         copy.wait_recv()
     from_state = jnp.where(
         opening, dot_nn(og_scaled[...], state_recv[...].reshape(channels, nstate)), 0.0
     )
-
-    for copy in gather_copies:
-        copy.wait_recv()
-    write_coeff = coeff[:, :nstate]
-    read_coeff = coeff[:, nstate:]
-    cg_partial[:, :nstate] = dot_nn(score_grad_t, read_coeff)
-    cg_partial[:, nstate:] = dot_nn(score_grad, write_coeff) + from_state
-    cg_send[...] = cg_partial[...].astype(BF16)
-    sum_copies = [
-        part_copy(2, j, cg_send.at[rows_of(lax.rem(f + j, parts))], cg_recv.at[j])
-        for j in range(1, parts)
-    ]
-    for copy in sum_copies:
-        copy.start()
-
-    open_read = jnp.where(opening, read_coeff.astype(F32), 0.0).astype(BF16)
-    sgrad_send[...] = (
-        dot_tn(og_scaled[...], open_read).astype(BF16).reshape(heads, docs, part_p, nstate)
-    )
-    sgrad_copies = [
-        doc_copy(2, j, sgrad_send.at[:, lax.rem(d + j, docs)], sgrad_recv.at[d])
-        for j in range(1, docs)
-    ]
-    for copy in sgrad_copies:
-        copy.start()
+    send_half(1, dot_nn(score_grad, write_coeff) + from_state)
+
     first_scores = dot_nt(write_coeff[:16], read_coeff)
     first_seg = jnp.broadcast_to(seg_row, (16, length)) == seg_cols[:16, :1]
     first_allowed = first_seg & (iota((16, length), 1) >= iota((16, length), 0))
@@ -550,27 +562,38 @@
         load.wait()
     tok_rows = tok_cols[...].T
 
-    for copy in sum_copies:
-        copy.wait_recv()
-    total = cg_partial[rows_of(f)]
-    for j in range(1, parts):
-        total = total + cg_recv[j].astype(F32)
-    cg[rows_of(f)] = total.astype(BF16)
-    cg_copies = [part_copy(3, j, cg.at[rows_of(f)], cg.at[rows_of(f)]) for j in range(1, parts)]
-    for copy in cg_copies:
-        copy.start()
-
-    for copy in cg_copies:
-        copy.wait_recv()
-    product = dot_nn(tok_rows, cg[...]).reshape(docs, out_rows, width)
-    fin_send[...] = product.astype(BF16)
-    fin_copies = [
-        doc_copy(4, j, fin_send.at[lax.rem(d + j, docs)], fin_recv.at[j - 1])
-        for j in range(1, docs)
-    ]
-    for copy in fin_copies:
-        copy.start()
-    fin_part[...] = product
+    cg_copies = [[], []]
+    for half in range(2):
+        columns = halves_of[half]
+        for copy in sum_copies[half]:
+            copy.wait_recv()
+        total = cg_partial[rows_of(f), columns]
+        for j in range(1, parts):
+            total = total + cg_recv[j, :, columns].astype(F32)
+        cg[rows_of(f), columns] = total.astype(BF16)
+        own = cg.at[rows_of(f), columns]
+        for j in range(1, parts):
+            copy = part_copy(4 + half, j, own, own)
+            copy.start()
+            cg_copies[half].append(copy)
+
+    fin_copies = []
+    for half in range(2):
+        columns = halves_of[half]
+        for copy in cg_copies[half]:
+            copy.wait_recv()
+        product = dot_nn(tok_rows, cg[:, columns]).reshape(docs, out_rows, nstate)
+        fin_send[:, :, columns] = product.astype(BF16)
+        for j in range(1, docs):
+            copy = doc_copy(
+                4 + half,
+                j,
+                fin_send.at[lax.rem(d + j, docs), :, columns],
+                fin_recv.at[j - 1, :, columns],
+            )
+            copy.start()
+            fin_copies.append(copy)
+        fin_part[:, :, columns] = product
     stores.append(pltpu.make_async_copy(fin_part.at[d], fin_own, store_sem.at[2]))
     stores[2].start()
     for copy in sgrad_copies + cgrad_copies + fin_copies:
@@ -583,10 +606,10 @@
         coeff_copies,
         state_copies,
         gather_copies,
-        sum_copies,
+        *sum_copies,
         sgrad_copies,
         cgrad_copies,
-        cg_copies,
+        *cg_copies,
         fin_copies,
     ):
         for copy in copies:
@@ -703,7 +726,8 @@
             pltpu.VMEM((length, depth), BF16),
             pltpu.VMEM((length, docs * out_rows), BF16),
             pltpu.VMEM((length, width), F32),
-            pltpu.VMEM((parts, block, width), F32),
+            pltpu.VMEM((length, width), BF16),
+            pltpu.VMEM((parts, block, width), BF16),
             pltpu.VMEM((length, width), BF16),
             pltpu.VMEM((length, width), F32),
             pltpu.VMEM((length, width), BF16),
@@ -725,10 +749,10 @@
             pltpu.VMEM((16, channels), F32),
             pltpu.SemaphoreType.DMA((11 + docs,)),
             pltpu.SemaphoreType.DMA((3,)),
-            pltpu.SemaphoreType.DMA((4, parts)),
-            pltpu.SemaphoreType.DMA((4, parts)),
-            pltpu.SemaphoreType.DMA((5, docs)),
-            pltpu.SemaphoreType.DMA((5, docs)),
+            pltpu.SemaphoreType.DMA((6, parts)),
+            pltpu.SemaphoreType.DMA((6, parts)),
+            pltpu.SemaphoreType.DMA((6, docs)),
+            pltpu.SemaphoreType.DMA((6, docs)),
         ],
         compiler_params=pltpu.CompilerParams(
             collective_id=0, has_side_effects=True, vmem_limit_bytes=60 * 1024 * 1024

time: 31.9 us -> 32.4 us (1.016)
  Pallas kernels: 31.1 us -> 31.6 us
    pallas_call x1, Pallas kernels: 29.1 us -> 29.6 us  [device_part(): pl.pallas_call(functools.partial(layer_kernel, docs, parts), out_shape=la...]
where the time goes in v4:
time: 32.4 us; the launch traced here: 32.2 us
  Pallas kernels  31.6 us (98%)
  between operations  0.64 us (2%)
    pallas_call x1, Pallas kernels, device_part(): pl.pallas_call(functools.partial(layer_kernel, docs, parts), out_shape=la...  29.6 us
    pallas_call x1, Pallas kernels, device_part(): pl.pallas_call(finish_kernel, out_shape=(jax.ShapeDtypeStruct((out_rows,...  1.95 us

profile of v4, /device:TPU:0, one launch (start us, length us, event | category | flops | bytes accessed | tf_op | source)
XLA Modules:
  0.0 32.2 jit_solution(11221507139207746038)
XLA Ops:
  0.6 29.6 %shard_map.130 = (f32[128,256]{1,0:T(8,128)}, bf16[3,128,256]{2,1,0:T(8,128)(2,1)}, bf16[4,16,16,128]{3,2,1,0:T(8,128)(2,1)}, bf16[4,3,16,16]{3,2,1,0:T(8,128)(2,1)}) custom-call(s32[4]{0:T(128)} %carry_hbm.3, bf16[1,256,4096]{2,1,0:T(8,128)(2,1)} %tokens_hbm.1, bf16[1,256,1024]{2,1,0:T(8,128)(2,1)} %mix_hbm.1, f32[1,16,256]{2,1,0:T(8,128)} %bitcast.2, ...), custom_call_target="tpu_custom_call" | custom-call | flops 536870912 | bytes 4194304 | tf_op jit(solution)/shard_map/pallas_call | solution.py:710
  30.2 2.0 %shard_map.131 = (f32[128,256]{1,0:T(8,128)}, bf16[4,16,16,128]{3,2,1,0:T(8,128)(2,1)}, bf16[4,3,16,16]{3,2,1,0:T(8,128)(2,1)}) custom-call(s32[4]{0:T(128)} %carry_hbm.3, f32[128,256]{1,0:T(8,128)} %get-tuple-element.7.own_hbm, bf16[3,128,256]{2,1,0:T(8,128)(2,1)} %get-tuple-element.8.recv_hbm, bf16[4,16,16,128]{3,2,1,0:T(8,128)(2,1)} %get-tuple-element.9.sgrad_hbm, ...), custom_call_target="tpu_custom_call" | custom-call | tf_op jit(solution)/shard_map/pallas_call | solution.py:776

commit v5 on v3

--- a/solution.py
+++ b/solution.py
@@ -249,8 +249,9 @@
     seg_ext,
     og_scaled,
     val_scaled,
-    first_step,
-    first_shrink,
+    first_scale,
+    tap_mask,
+    factors,
     load_sem,
     store_sem,
     part_send_sem,
@@ -333,15 +334,11 @@
     lane = iota((1, channels), 1)
     head_of_lane = lax.div(lane, head_dim)
     lane_in_head = lane - head_of_lane * head_dim
-    places = [
-        jnp.where(
-            jnp.broadcast_to(lane_in_head, (part_p, channels))
-            == iota((part_p, channels), 0) + q * part_p,
-            1.0,
-            0.0,
-        ).astype(BF16)
-        for q in range(docs)
-    ]
+    place = jnp.where(
+        jnp.broadcast_to(lane_in_head, (head_dim, channels)) == iota((head_dim, channels), 0),
+        1.0,
+        0.0,
+    ).astype(BF16)
     head_rows = (taps - 1) * heads
     own_head = jnp.broadcast_to(head_of_lane, (heads, channels)) == iota((heads, channels), 0)
 
@@ -385,13 +382,16 @@
         keepdims=True,
     )
     steps = step_ref[...]
-    log_decay = lax.dot_general(
-        -(rate * steps),
-        jnp.where(lower, 1.0, 0.0),
-        (((1,), (1,)), ((), ())),
-        precision=lax.Precision.HIGHEST,
-        preferred_element_type=F32,
-    )
+    rest = -(rate * steps)
+    pieces = []
+    for _ in range(3):
+        piece = rest.astype(BF16)
+        pieces.append(piece)
+        rest = rest - piece.astype(F32)
+    sums = dot_nt(
+        jnp.concatenate(pieces, axis=0), jnp.where(lower, 1.0, 0.0).astype(BF16)
+    )
+    log_decay = sums[:heads] + sums[heads : 2 * heads] + sums[2 * heads :]
 
     def halves(x):
         top = x.astype(BF16).astype(F32)
@@ -399,8 +399,7 @@
         return both.T.astype(BF16)
 
     grow = halves(jnp.exp(log_decay))
-    shrink = halves(jnp.exp(-log_decay))
-    step_halves = halves(steps)
+    shrink = halves(steps * jnp.exp(-log_decay))
 
     seg_row = seg_ref[...].astype(F32)
     seg_cols = jnp.broadcast_to(seg_row, (128, length)).T
@@ -408,10 +407,11 @@
     seg_ext[:8, :] = jnp.broadcast_to(seg_cols[:1], (8, 128))
     opening = seg_cols == seg_cols[:1]
 
-    def scaled_values(preact, step, shrink_factor):
-        mixed = (preact / (1.0 + jnp.exp(-preact))).astype(BF16).astype(F32)
-        values = (step * mixed).astype(BF16).astype(F32)
-        return (values * shrink_factor).astype(BF16)
+    for k in range(1, taps):
+        tap_mask[k - 1] = jnp.where(seg_ext[8 - k : 8 - k + length, :] == seg_cols, 1.0, 0.0)
+
+    def scaled_values(preact, factor):
+        return (preact * (0.5 + 0.5 * jnp.tanh(0.5 * preact)) * factor).astype(BF16)
 
     ext[:8, :] = jnp.zeros((8, channels), F32)
 
@@ -427,17 +427,19 @@
             return dot_nn(both, expand)
 
         ext[8:, lanes] = mix_ref[:, lanes].astype(F32)
-        preact = jnp.zeros((length, 128), F32)
-        for k in range(taps):
-            same = seg_ext[8 - k : 8 - k + length, :] == seg_cols
-            window = ext[8 - k : 8 - k + length, lanes]
-            preact = preact + jnp.where(same, taps_ref[k : k + 1, lanes] * window, 0.0)
-        step_c = per_channel(step_halves)
-        shrink_c = per_channel(shrink)
-        val_scaled[:, lanes] = scaled_values(preact, step_c, shrink_c)
-        og_scaled[:, lanes] = (grad_ref[:, lanes].astype(F32) * per_channel(grow)).astype(BF16)
-        first_step[:, lanes] = step_c[:16]
-        first_shrink[:, lanes] = shrink_c[:16]
+        factors[0] = per_channel(grow)
+        factors[1] = per_channel(shrink)
+        first_scale[:, lanes] = factors[1, :16, :]
+        for base in range(0, length, 64):
+            rows = slice(base, base + 64)
+            preact = taps_ref[0:1, lanes] * ext[8 + base : 72 + base, lanes]
+            for k in range(1, taps):
+                window = ext[8 - k + base : 72 - k + base, lanes]
+                preact = preact + taps_ref[k : k + 1, lanes] * (tap_mask[k - 1, rows, :] * window)
+            val_scaled[rows, lanes] = scaled_values(preact, factors[1, rows, :])
+            og_scaled[rows, lanes] = (
+                grad_ref[rows, lanes].astype(F32) * factors[0, rows, :]
+            ).astype(BF16)
         return carry
 
     chunks = channels // 128
@@ -460,9 +462,12 @@
     for copy in conv_copies:
         copy.wait_recv()
 
-    spread = jnp.zeros((head_rows, channels), F32)
-    for q in range(docs):
-        spread = spread + dot_nn(conv_recv[q].reshape(head_rows, part_p), places[q])
+    spread = dot_nn(
+        jnp.concatenate(
+            [conv_recv[q].reshape(head_rows, part_p) for q in range(docs)], axis=1
+        ),
+        place,
+    )
     carried_rows = jnp.sum(
         jnp.where(own_head[None], spread.reshape(taps - 1, heads, channels), 0.0), axis=1
     )
@@ -472,16 +477,13 @@
         same = seg_ext[8 - k : 24 - k, :1] == seg_cols[:16, :1]
         window = ext[8 - k : 24 - k, :]
         pre = pre + jnp.where(same, taps_ref[k : k + 1, :] * window, 0.0)
-    val_scaled[:16, :] = scaled_values(pre, first_step[...], first_shrink[...])
-
-    upper = iota((length, length), 0) <= iota((length, length), 1)
+    val_scaled[:16, :] = scaled_values(pre, first_scale[...])
+
     same_doc = seg_cols[:, :1] == seg_row
     score_grad = jnp.where(
         lower & same_doc, dot_nt(og_scaled[...], val_scaled[...]), 0.0
     ).astype(BF16)
-    score_grad_t = jnp.where(
-        upper & same_doc, dot_nt(val_scaled[...], og_scaled[...]), 0.0
-    ).astype(BF16)
+    score_grad_t = score_grad.T
 
     for copy in state_copies:
         copy.wait_recv()
@@ -513,6 +515,24 @@
     ]
     for copy in sgrad_copies:
         copy.start()
+    stores = [
+        pltpu.make_async_copy(sgrad_send.at[:, d], sgrad_recv.at[d], store_sem.at[0]),
+    ]
+    stores[0].start()
+    for load in loads[11:]:
+        load.wait()
+    tok_rows = tok_cols[...].T
+
+    for copy in sum_copies:
+        copy.wait_recv()
+    total = cg_partial[rows_of(f)]
+    for j in range(1, parts):
+        total = total + cg_recv[j].astype(F32)
+    cg[rows_of(f)] = total.astype(BF16)
+    cg_copies = [part_copy(3, j, cg.at[rows_of(f)], cg.at[rows_of(f)]) for j in range(1, parts)]
+    for copy in cg_copies:
+        copy.start()
+
     first_scores = dot_nt(write_coeff[:16], read_coeff)
     first_seg = jnp.broadcast_to(seg_row, (16, length)) == seg_cols[:16, :1]
     first_allowed = first_seg & (iota((16, length), 1) >= iota((16, length), 0))
@@ -520,7 +540,7 @@
     first_grad = dot_nn(first_scores, og_scaled[...])[:8]
     pre = pre[:8]
     gate = 1.0 / (1.0 + jnp.exp(-pre))
-    pre_grad = first_grad * first_step[:8] * first_shrink[:8] * gate * (1.0 + pre * (1.0 - gate))
+    pre_grad = first_grad * first_scale[:8] * gate * (1.0 + pre * (1.0 - gate))
     pre_grad = jnp.where(seg_cols[:8, :1] == seg_cols[:1, :1], pre_grad, 0.0)
     conv_rows = []
     for row in range(taps - 1):
@@ -531,34 +551,19 @@
         conv_rows.append(
             jnp.where(own_head, jnp.broadcast_to(running, (heads, channels)), 0.0).astype(BF16)
         )
+    placed = dot_nt(jnp.concatenate(conv_rows, axis=0), place).astype(BF16)
     for q in range(docs):
-        for row in range(taps - 1):
-            cgrad_send[q, row] = dot_nt(conv_rows[row], places[q]).astype(BF16)
+        cgrad_send[q] = placed[:, q * part_p : (q + 1) * part_p].reshape(
+            taps - 1, heads, part_p
+        )
     cgrad_copies = [
         doc_copy(3, j, cgrad_send.at[lax.rem(d + j, docs)], cgrad_recv.at[d])
         for j in range(1, docs)
     ]
     for copy in cgrad_copies:
         copy.start()
-    stores = [
-        pltpu.make_async_copy(sgrad_send.at[:, d], sgrad_recv.at[d], store_sem.at[0]),
-        pltpu.make_async_copy(cgrad_send.at[d], cgrad_recv.at[d], store_sem.at[1]),
-    ]
-    for store in stores:
-        store.start()
-    for load in loads[11:]:
-        load.wait()
-    tok_rows = tok_cols[...].T
-
-    for copy in sum_copies:
-        copy.wait_recv()
-    total = cg_partial[rows_of(f)]
-    for j in range(1, parts):
-        total = total + cg_recv[j].astype(F32)
-    cg[rows_of(f)] = total.astype(BF16)
-    cg_copies = [part_copy(3, j, cg.at[rows_of(f)], cg.at[rows_of(f)]) for j in range(1, parts)]
-    for copy in cg_copies:
-        copy.start()
+    stores.append(pltpu.make_async_copy(cgrad_send.at[d], cgrad_recv.at[d], store_sem.at[1]))
+    stores[1].start()
 
     for copy in cg_copies:
         copy.wait_recv()
@@ -668,6 +673,7 @@
         and heads % 16 == 0
         and 2 * heads <= 128
         and block % 16 == 0
+        and length % 64 == 0
         and out_rows % 128 == 0
         and depth % 128 == 0
         and nstate == 128
@@ -722,7 +728,8 @@
             pltpu.VMEM((length, channels), BF16),
             pltpu.VMEM((length, channels), BF16),
             pltpu.VMEM((16, channels), F32),
-            pltpu.VMEM((16, channels), F32),
+            pltpu.VMEM((taps - 1, length, 128), F32),
+            pltpu.VMEM((2, length, 128), F32),
             pltpu.SemaphoreType.DMA((11 + docs,)),
             pltpu.SemaphoreType.DMA((3,)),
             pltpu.SemaphoreType.DMA((4, parts)),

time: 31.9 us -> 31.9 us (level)
  no operation moved by 1% of the time
where the time goes in v5:
time: 31.9 us; the launch traced here: 31.7 us
  Pallas kernels  31.1 us (97%)
  between operations  0.64 us (2%)
    pallas_call x1, Pallas kernels, device_part(): pl.pallas_call(functools.partial(layer_kernel, docs, parts), out_shape=la...  29.1 us
    pallas_call x1, Pallas kernels, device_part(): pl.pallas_call(finish_kernel, out_shape=(jax.ShapeDtypeStruct((out_rows,...  1.95 us

profile of v5, /device:TPU:0, one launch (start us, length us, event | category | flops | bytes accessed | tf_op | source)
XLA Modules:
  0.0 31.7 jit_solution(1212974035358702310)
XLA Ops:
  0.6 29.1 %shard_map.130 = (f32[128,256]{1,0:T(8,128)}, bf16[3,128,256]{2,1,0:T(8,128)(2,1)}, bf16[4,16,16,128]{3,2,1,0:T(8,128)(2,1)}, bf16[4,3,16,16]{3,2,1,0:T(8,128)(2,1)}) custom-call(s32[4]{0:T(128)} %carry_hbm.3, bf16[1,256,4096]{2,1,0:T(8,128)(2,1)} %tokens_hbm.1, bf16[1,256,1024]{2,1,0:T(8,128)(2,1)} %mix_hbm.1, f32[1,16,256]{2,1,0:T(8,128)} %bitcast.2, ...), custom_call_target="tpu_custom_call" | custom-call | flops 536870912 | bytes 4194304 | tf_op jit(solution)/shard_map/pallas_call | solution.py:693
  29.8 2.0 %shard_map.131 = (f32[128,256]{1,0:T(8,128)}, bf16[4,16,16,128]{3,2,1,0:T(8,128)(2,1)}, bf16[4,3,16,16]{3,2,1,0:T(8,128)(2,1)}) custom-call(s32[4]{0:T(128)} %carry_hbm.3, f32[128,256]{1,0:T(8,128)} %get-tuple-element.7.own_hbm, bf16[3,128,256]{2,1,0:T(8,128)(2,1)} %get-tuple-element.8.recv_hbm, bf16[4,16,16,128]{3,2,1,0:T(8,128)(2,1)} %get-tuple-element.9.sgrad_hbm, ...), custom_call_target="tpu_custom_call" | custom-call | tf_op jit(solution)/shard_map/pallas_call | solution.py:759

commit v6 on v5

--- a/solution.py
+++ b/solution.py
@@ -245,6 +245,8 @@
     cgrad_send,
     fin_part,
     fin_send,
+    fin_pair,
+    fin_cross,
     ext,
     seg_ext,
     og_scaled,
@@ -569,16 +571,34 @@
         copy.wait_recv()
     product = dot_nn(tok_rows, cg[...]).reshape(docs, out_rows, width)
     fin_send[...] = product.astype(BF16)
+    fin_part[...] = product
+    near = d + 1 - 2 * lax.rem(d, 2)
+    far = lax.rem(d + docs // 2, docs)
+    near_far = lax.rem(near + docs // 2, docs)
+
+    def fin_copy(k, src, dst, target):
+        return pltpu.make_async_remote_copy(
+            src_ref=src,
+            dst_ref=dst,
+            send_sem=doc_send_sem.at[4, k],
+            recv_sem=doc_recv_sem.at[4, k],
+            device_id=(target, f),
+            device_id_type=MESH,
+        )
+
     fin_copies = [
-        doc_copy(4, j, fin_send.at[lax.rem(d + j, docs)], fin_recv.at[j - 1])
-        for j in range(1, docs)
+        fin_copy(0, fin_send.at[near_far], fin_pair, near),
+        fin_copy(1, fin_send.at[near], fin_recv.at[0], near),
     ]
     for copy in fin_copies:
         copy.start()
-    fin_part[...] = product
+    fin_copies[0].wait_recv()
+    fin_cross[...] = (fin_part[far] + fin_pair[...].astype(F32)).astype(BF16)
+    fin_copies.append(fin_copy(2, fin_cross, fin_recv.at[1], far))
+    fin_copies[2].start()
     stores.append(pltpu.make_async_copy(fin_part.at[d], fin_own, store_sem.at[2]))
     stores[2].start()
-    for copy in sgrad_copies + cgrad_copies + fin_copies:
+    for copy in sgrad_copies + cgrad_copies + fin_copies[1:]:
         copy.wait_recv()
     for store in stores:
         store.wait()
@@ -669,6 +689,7 @@
     aligned = (
         rows_dev == 1
         and slots == docs
+        and docs == 4
         and part_p % 16 == 0
         and heads % 16 == 0
         and 2 * heads <= 128
@@ -686,7 +707,7 @@
     hbm = pl.BlockSpec(memory_space=pltpu.HBM)
     landed = (
         jax.ShapeDtypeStruct((out_rows, width), F32),
-        jax.ShapeDtypeStruct((docs - 1, out_rows, width), BF16),
+        jax.ShapeDtypeStruct((2, out_rows, width), BF16),
         jax.ShapeDtypeStruct(carried_state.shape, BF16),
         jax.ShapeDtypeStruct(carried_conv.shape, BF16),
     )
@@ -723,6 +744,8 @@
             pltpu.VMEM((docs, taps - 1, heads, part_p), BF16),
             pltpu.VMEM((docs, out_rows, width), F32),
             pltpu.VMEM((docs, out_rows, width), BF16),
+            pltpu.VMEM((out_rows, width), BF16),
+            pltpu.VMEM((out_rows, width), BF16),
             pltpu.VMEM((length + 8, channels), F32),
             pltpu.VMEM((length + 8, 128), F32),
             pltpu.VMEM((length, channels), BF16),

time: 31.9 us -> 34.3 us (1.075)
  Pallas kernels: 31.1 us -> 33.4 us
    pallas_call x1, Pallas kernels: 29.1 us -> 31.5 us  [device_part(): pl.pallas_call(functools.partial(layer_kernel, docs, parts), out_shape=la...]
where the time goes in v6:
time: 34.3 us; the launch traced here: 34.1 us
  Pallas kernels  33.4 us (97%)
  between operations  0.64 us (2%)
    pallas_call x1, Pallas kernels, device_part(): pl.pallas_call(functools.partial(layer_kernel, docs, parts), out_shape=la...  31.5 us
    pallas_call x1, Pallas kernels, device_part(): pl.pallas_call(finish_kernel, out_shape=(jax.ShapeDtypeStruct((out_rows,...  1.93 us

profile of v6, /device:TPU:0, one launch (start us, length us, event | category | flops | bytes accessed | tf_op | source)
XLA Modules:
  0.0 34.1 jit_solution(950937733475196752)
XLA Ops:
  0.6 31.5 %shard_map.130 = (f32[128,256]{1,0:T(8,128)}, bf16[2,128,256]{2,1,0:T(8,128)(2,1)}, bf16[4,16,16,128]{3,2,1,0:T(8,128)(2,1)}, bf16[4,3,16,16]{3,2,1,0:T(8,128)(2,1)}) custom-call(s32[4]{0:T(128)} %carry_hbm.3, bf16[1,256,4096]{2,1,0:T(8,128)(2,1)} %tokens_hbm.1, bf16[1,256,1024]{2,1,0:T(8,128)(2,1)} %mix_hbm.1, f32[1,16,256]{2,1,0:T(8,128)} %bitcast.2, ...), custom_call_target="tpu_custom_call" | custom-call | flops 536870912 | bytes 4194304 | tf_op jit(solution)/shard_map/pallas_call | solution.py:714
  32.2 1.9 %shard_map.131 = (f32[128,256]{1,0:T(8,128)}, bf16[4,16,16,128]{3,2,1,0:T(8,128)(2,1)}, bf16[4,3,16,16]{3,2,1,0:T(8,128)(2,1)}) custom-call(s32[4]{0:T(128)} %carry_hbm.3, f32[128,256]{1,0:T(8,128)} %get-tuple-element.7.own_hbm, bf16[2,128,256]{2,1,0:T(8,128)(2,1)} %get-tuple-element.8.recv_hbm, bf16[4,16,16,128]{3,2,1,0:T(8,128)(2,1)} %get-tuple-element.9.sgrad_hbm, ...), custom_call_target="tpu_custom_call" | custom-call | tf_op jit(solution)/shard_map/pallas_call | solution.py:782

commit v7 on v5

--- a/solution.py
+++ b/solution.py
@@ -233,10 +233,10 @@
     coeff_partial,
     coeff_recv,
     coeff,
-    cg_partial,
-    cg_send,
-    cg_recv,
-    cg,
+    sum_partial,
+    sum_send,
+    sum_recv,
+    sums_of,
     state_send,
     state_recv,
     conv_send,
@@ -443,7 +443,7 @@
         return carry
 
     chunks = channels // 128
-    lax.fori_loop(0, chunks // 2, chunk, 0)
+    lax.fori_loop(0, chunks, chunk, 0)
 
     for copy in coeff_copies:
         copy.wait_recv()
@@ -457,7 +457,6 @@
     for copy in gather_copies:
         copy.start()
 
-    lax.fori_loop(chunks // 2, chunks, chunk, 0)
 
     for copy in conv_copies:
         copy.wait_recv()
@@ -480,30 +479,28 @@
     val_scaled[:16, :] = scaled_values(pre, first_scale[...])
 
     same_doc = seg_cols[:, :1] == seg_row
-    score_grad = jnp.where(
-        lower & same_doc, dot_nt(og_scaled[...], val_scaled[...]), 0.0
-    ).astype(BF16)
-    score_grad_t = score_grad.T
-
+    score_grad = jnp.where(lower & same_doc, dot_nt(og_scaled[...], val_scaled[...]), 0.0)
+    sum_partial[:, :length] = score_grad
+    sum_send[:, :length] = score_grad.astype(BF16)
     for copy in state_copies:
         copy.wait_recv()
     from_state = jnp.where(
         opening, dot_nn(og_scaled[...], state_recv[...].reshape(channels, nstate)), 0.0
     )
+    sum_partial[:, length:] = from_state
+    sum_send[:, length:] = from_state.astype(BF16)
+
+    sum_copies = [
+        part_copy(2, j, sum_send.at[rows_of(lax.rem(f + j, parts))], sum_recv.at[j])
+        for j in range(1, parts)
+    ]
+    for copy in sum_copies:
+        copy.start()
 
     for copy in gather_copies:
         copy.wait_recv()
     write_coeff = coeff[:, :nstate]
     read_coeff = coeff[:, nstate:]
-    cg_partial[:, :nstate] = dot_nn(score_grad_t, read_coeff)
-    cg_partial[:, nstate:] = dot_nn(score_grad, write_coeff) + from_state
-    cg_send[...] = cg_partial[...].astype(BF16)
-    sum_copies = [
-        part_copy(2, j, cg_send.at[rows_of(lax.rem(f + j, parts))], cg_recv.at[j])
-        for j in range(1, parts)
-    ]
-    for copy in sum_copies:
-        copy.start()
 
     open_read = jnp.where(opening, read_coeff.astype(F32), 0.0).astype(BF16)
     sgrad_send[...] = (
@@ -525,12 +522,14 @@
 
     for copy in sum_copies:
         copy.wait_recv()
-    total = cg_partial[rows_of(f)]
+    total = sum_partial[rows_of(f)]
     for j in range(1, parts):
-        total = total + cg_recv[j].astype(F32)
-    cg[rows_of(f)] = total.astype(BF16)
-    cg_copies = [part_copy(3, j, cg.at[rows_of(f)], cg.at[rows_of(f)]) for j in range(1, parts)]
-    for copy in cg_copies:
+        total = total + sum_recv[j].astype(F32)
+    sums_of[rows_of(f)] = total.astype(BF16)
+    total_copies = [
+        part_copy(3, j, sums_of.at[rows_of(f)], sums_of.at[rows_of(f)]) for j in range(1, parts)
+    ]
+    for copy in total_copies:
         copy.start()
 
     first_scores = dot_nt(write_coeff[:16], read_coeff)
@@ -565,9 +564,13 @@
     stores.append(pltpu.make_async_copy(cgrad_send.at[d], cgrad_recv.at[d], store_sem.at[1]))
     stores[1].start()
 
-    for copy in cg_copies:
+    for copy in total_copies:
         copy.wait_recv()
-    product = dot_nn(tok_rows, cg[...]).reshape(docs, out_rows, width)
+    score_total = sums_of[:, :length]
+    write_grad = dot_tn(score_total, read_coeff)
+    read_grad = dot_nn(score_total, write_coeff) + sums_of[:, length:].astype(F32)
+    cg = jnp.concatenate([write_grad, read_grad], axis=1).astype(BF16)
+    product = dot_nn(tok_rows, cg).reshape(docs, out_rows, width)
     fin_send[...] = product.astype(BF16)
     fin_copies = [
         doc_copy(4, j, fin_send.at[lax.rem(d + j, docs)], fin_recv.at[j - 1])
@@ -591,7 +594,7 @@
         sum_copies,
         sgrad_copies,
         cgrad_copies,
-        cg_copies,
+        total_copies,
         fin_copies,
     ):
         for copy in copies:
@@ -673,7 +676,7 @@
         and heads % 16 == 0
         and 2 * heads <= 128
         and block % 16 == 0
-        and length % 64 == 0
+        and length % 128 == 0
         and out_rows % 128 == 0
         and depth % 128 == 0
         and nstate == 128
@@ -711,10 +714,10 @@
             pltpu.VMEM((length, width), F32),
             pltpu.VMEM((parts, block, width), F32),
             pltpu.VMEM((length, width), BF16),
-            pltpu.VMEM((length, width), F32),
-            pltpu.VMEM((length, width), BF16),
-            pltpu.VMEM((parts, block, width), BF16),
-            pltpu.VMEM((length, width), BF16),
+            pltpu.VMEM((length, length + nstate), F32),
+            pltpu.VMEM((length, length + nstate), BF16),
+            pltpu.VMEM((parts, block, length + nstate), BF16),
+            pltpu.VMEM((length, length + nstate), BF16),
             pltpu.VMEM((slots, heads, part_p, nstate), BF16),
             pltpu.VMEM((heads, docs, part_p, nstate), BF16),
             pltpu.VMEM((slots, taps - 1, heads, part_p), BF16),

time: 31.9 us -> 32.7 us (1.025)
  Pallas kernels: 31.1 us -> 31.8 us
    pallas_call x1, Pallas kernels: 29.1 us -> 29.9 us  [device_part(): pl.pallas_call(functools.partial(layer_kernel, docs, parts), out_shape=la...]
where the time goes in v7:
time: 32.7 us; the launch traced here: 32.5 us
  Pallas kernels  31.8 us (97%)
  between operations  0.64 us (2%)
    pallas_call x1, Pallas kernels, device_part(): pl.pallas_call(functools.partial(layer_kernel, docs, parts), out_shape=la...  29.9 us
    pallas_call x1, Pallas kernels, device_part(): pl.pallas_call(finish_kernel, out_shape=(jax.ShapeDtypeStruct((out_rows,...  1.95 us

profile of v7, /device:TPU:0, one launch (start us, length us, event | category | flops | bytes accessed | tf_op | source)
XLA Modules:
  0.0 32.5 jit_solution(2781954522546073988)
XLA Ops:
  0.6 29.9 %shard_map.130 = (f32[128,256]{1,0:T(8,128)}, bf16[3,128,256]{2,1,0:T(8,128)(2,1)}, bf16[4,16,16,128]{3,2,1,0:T(8,128)(2,1)}, bf16[4,3,16,16]{3,2,1,0:T(8,128)(2,1)}) custom-call(s32[4]{0:T(128)} %carry_hbm.3, bf16[1,256,4096]{2,1,0:T(8,128)(2,1)} %tokens_hbm.1, bf16[1,256,1024]{2,1,0:T(8,128)(2,1)} %mix_hbm.1, f32[1,16,256]{2,1,0:T(8,128)} %bitcast.2, ...), custom_call_target="tpu_custom_call" | custom-call | flops 536870912 | bytes 4194304 | tf_op jit(solution)/shard_map/pallas_call | solution.py:696
  30.5 2.0 %shard_map.131 = (f32[128,256]{1,0:T(8,128)}, bf16[4,16,16,128]{3,2,1,0:T(8,128)(2,1)}, bf16[4,3,16,16]{3,2,1,0:T(8,128)(2,1)}) custom-call(s32[4]{0:T(128)} %carry_hbm.3, f32[128,256]{1,0:T(8,128)} %get-tuple-element.7.own_hbm, bf16[3,128,256]{2,1,0:T(8,128)(2,1)} %get-tuple-element.8.recv_hbm, bf16[4,16,16,128]{3,2,1,0:T(8,128)(2,1)} %get-tuple-element.9.sgrad_hbm, ...), custom_call_target="tpu_custom_call" | custom-call | tf_op jit(solution)/shard_map/pallas_call | solution.py:762

commit v8 on v7

--- a/solution.py
+++ b/solution.py
@@ -415,35 +415,30 @@
 
     ext[:8, :] = jnp.zeros((8, channels), F32)
 
-    def chunk(c, carry):
-        lanes = pl.ds(pl.multiple_of(c * 128, 128), 128)
-        row = iota((128, 128), 0)
-        head = jnp.broadcast_to(
-            lax.div(iota((1, 128), 1) + c * 128, head_dim), (128, 128)
-        )
-        expand = jnp.where((row == head) | (row == head + heads), 1.0, 0.0).astype(BF16)
-
-        def per_channel(both):
-            return dot_nn(both, expand)
-
+    row = iota((128, channels), 0)
+    head = jnp.broadcast_to(head_of_lane, (128, channels))
+    expand = jnp.where((row == head) | (row == head + heads), 1.0, 0.0).astype(BF16)
+    factors[0] = dot_nn(grow, expand)
+    factors[1] = dot_nn(shrink, expand)
+    first_scale[...] = factors[1, :16, :]
+
+    def chunk(c):
+        lanes = slice(c * 128, (c + 1) * 128)
         ext[8:, lanes] = mix_ref[:, lanes].astype(F32)
-        factors[0] = per_channel(grow)
-        factors[1] = per_channel(shrink)
-        first_scale[:, lanes] = factors[1, :16, :]
         for base in range(0, length, 64):
             rows = slice(base, base + 64)
             preact = taps_ref[0:1, lanes] * ext[8 + base : 72 + base, lanes]
             for k in range(1, taps):
                 window = ext[8 - k + base : 72 - k + base, lanes]
                 preact = preact + taps_ref[k : k + 1, lanes] * (tap_mask[k - 1, rows, :] * window)
-            val_scaled[rows, lanes] = scaled_values(preact, factors[1, rows, :])
+            val_scaled[rows, lanes] = scaled_values(preact, factors[1, rows, lanes])
             og_scaled[rows, lanes] = (
-                grad_ref[rows, lanes].astype(F32) * factors[0, rows, :]
+                grad_ref[rows, lanes].astype(F32) * factors[0, rows, lanes]
             ).astype(BF16)
-        return carry
 
     chunks = channels // 128
-    lax.fori_loop(0, chunks, chunk, 0)
+    for c in range(chunks // 2):
+        chunk(c)
 
     for copy in coeff_copies:
         copy.wait_recv()
@@ -458,6 +453,9 @@
         copy.start()
 
 
+    for c in range(chunks // 2, chunks):
+        chunk(c)
+
     for copy in conv_copies:
         copy.wait_recv()
 
@@ -497,25 +495,6 @@
     for copy in sum_copies:
         copy.start()
 
-    for copy in gather_copies:
-        copy.wait_recv()
-    write_coeff = coeff[:, :nstate]
-    read_coeff = coeff[:, nstate:]
-
-    open_read = jnp.where(opening, read_coeff.astype(F32), 0.0).astype(BF16)
-    sgrad_send[...] = (
-        dot_tn(og_scaled[...], open_read).astype(BF16).reshape(heads, docs, part_p, nstate)
-    )
-    sgrad_copies = [
-        doc_copy(2, j, sgrad_send.at[:, lax.rem(d + j, docs)], sgrad_recv.at[d])
-        for j in range(1, docs)
-    ]
-    for copy in sgrad_copies:
-        copy.start()
-    stores = [
-        pltpu.make_async_copy(sgrad_send.at[:, d], sgrad_recv.at[d], store_sem.at[0]),
-    ]
-    stores[0].start()
     for load in loads[11:]:
         load.wait()
     tok_rows = tok_cols[...].T
@@ -532,6 +511,25 @@
     for copy in total_copies:
         copy.start()
 
+    for copy in gather_copies:
+        copy.wait_recv()
+    write_coeff = coeff[:, :nstate]
+    read_coeff = coeff[:, nstate:]
+
+    open_read = jnp.where(opening, read_coeff.astype(F32), 0.0).astype(BF16)
+    sgrad_send[...] = (
+        dot_tn(og_scaled[...], open_read).astype(BF16).reshape(heads, docs, part_p, nstate)
+    )
+    sgrad_copies = [
+        doc_copy(2, j, sgrad_send.at[:, lax.rem(d + j, docs)], sgrad_recv.at[d])
+        for j in range(1, docs)
+    ]
+    for copy in sgrad_copies:
+        copy.start()
+    stores = [
+        pltpu.make_async_copy(sgrad_send.at[:, d], sgrad_recv.at[d], store_sem.at[0]),
+    ]
+    stores[0].start()
     first_scores = dot_nt(write_coeff[:16], read_coeff)
     first_seg = jnp.broadcast_to(seg_row, (16, length)) == seg_cols[:16, :1]
     first_allowed = first_seg & (iota((16, length), 1) >= iota((16, length), 0))
@@ -732,7 +730,7 @@
             pltpu.VMEM((length, channels), BF16),
             pltpu.VMEM((16, channels), F32),
             pltpu.VMEM((taps - 1, length, 128), F32),
-            pltpu.VMEM((2, length, 128), F32),
+            pltpu.VMEM((2, length, channels), F32),
             pltpu.SemaphoreType.DMA((11 + docs,)),
             pltpu.SemaphoreType.DMA((3,)),
             pltpu.SemaphoreType.DMA((4, parts)),

time: 32.7 us -> 35.1 us (1.073)
  Pallas kernels: 31.8 us -> 34.3 us
    pallas_call x1, Pallas kernels: 29.9 us -> 32.3 us  [device_part(): pl.pallas_call(functools.partial(layer_kernel, docs, parts), out_shape=la...]
where the time goes in v8:
time: 35.1 us; the launch traced here: 34.9 us
  Pallas kernels  34.3 us (98%)
  between operations  0.64 us (2%)
    pallas_call x1, Pallas kernels, device_part(): pl.pallas_call(functools.partial(layer_kernel, docs, parts), out_shape=la...  32.3 us
    pallas_call x1, Pallas kernels, device_part(): pl.pallas_call(finish_kernel, out_shape=(jax.ShapeDtypeStruct((out_rows,...  1.95 us

profile of v8, /device:TPU:0, one launch (start us, length us, event | category | flops | bytes accessed | tf_op | source)
XLA Modules:
  0.0 34.9 jit_solution(3466386885805462547)
XLA Ops:
  0.6 32.3 %shard_map.130 = (f32[128,256]{1,0:T(8,128)}, bf16[3,128,256]{2,1,0:T(8,128)(2,1)}, bf16[4,16,16,128]{3,2,1,0:T(8,128)(2,1)}, bf16[4,3,16,16]{3,2,1,0:T(8,128)(2,1)}) custom-call(s32[4]{0:T(128)} %carry_hbm.3, bf16[1,256,4096]{2,1,0:T(8,128)(2,1)} %tokens_hbm.1, bf16[1,256,1024]{2,1,0:T(8,128)(2,1)} %mix_hbm.1, f32[1,16,256]{2,1,0:T(8,128)} %bitcast.2, ...), custom_call_target="tpu_custom_call" | custom-call | flops 536870912 | bytes 4194304 | tf_op jit(solution)/shard_map/pallas_call | solution.py:694
  33.0 2.0 %shard_map.131 = (f32[128,256]{1,0:T(8,128)}, bf16[4,16,16,128]{3,2,1,0:T(8,128)(2,1)}, bf16[4,3,16,16]{3,2,1,0:T(8,128)(2,1)}) custom-call(s32[4]{0:T(128)} %carry_hbm.3, f32[128,256]{1,0:T(8,128)} %get-tuple-element.7.own_hbm, bf16[3,128,256]{2,1,0:T(8,128)(2,1)} %get-tuple-element.8.recv_hbm, bf16[4,16,16,128]{3,2,1,0:T(8,128)(2,1)} %get-tuple-element.9.sgrad_hbm, ...), custom_call_target="tpu_custom_call" | custom-call | tf_op jit(solution)/shard_map/pallas_call | solution.py:760
